TPU v7x, 32 devices: a whole 2x2x4 slice. The times are simulated.
32 devices in a mesh: ens: 2 (over x), tile: 16 (over z, y, core).
Axes of the slice: x: 2, y: 2, z: 4, core: 2. Of those that a mesh axis runs over, the one named last changes fastest.
Arguments:
- departure: float32 [131072], P(('ens', 'tile')), parts along dimension 0, may hold values from -6 to 6
- obs_weight: float32 [131072], P(('ens', 'tile')), parts along dimension 0, may hold values from 1 to 10
- owner_id: int32 [131072, 1], P(('ens', 'tile')), parts along dimension 0, may hold values from 0 to 15; in each aligned block of 4096 rows (0 to 4095, 4096 to 8191, ...) at most 512 rows name the same one
- obs_level: int32 [131072], P(('ens', 'tile')), parts along dimension 0, may hold values from 0 to 126
- columns: int32 [4, 131072], P(None, ('ens', 'tile')), parts along dimension 1, may hold values from 0 to 4095, as said below
- interp_weight: float32 [4, 131072], P(None, ('ens', 'tile')), parts along dimension 1, may hold values from 0 to 1, as said below
- vert_root: float32 [127, 127], replicated, may hold values from -0.5 to 0.5
- spread: float32 [256, 256], P('tile'), may hold values from 0.05 to 0.24
- lanczos: float32 [127, 512, 256], P(None, ('ens', 'tile')), parts along dimension 1, may hold values from -70 to 70
- previous: float32 [127, 512, 256], P(None, ('ens', 'tile')), parts along dimension 1, may hold values from -6 to 6
- beta_prev: float32 [2], P('ens'), parts along dimension 0, may hold values from 0.3 to 1.5
Outputs:
- next_vector: float32 [127, 512, 256], P(None, ('ens', 'tile')), parts along dimension 1
- coefficients: float32 [4], P('ens'), parts along dimension 0
There are 2 independent parts, one for each index of `ens`. A program takes and returns all parts, laid end to end along the dimension named above; an argument that names none is the same for every part. Nothing has to cross between parts.
Inputs may be any that keep to these rules, and one draw needn't show every extreme that they name: `owner_id`: in the rows of one device at most 512 observations name one owner; some owner is named by exactly 512 of them. `columns`: the four entries of an observation are the corners of one cell of the owner's rows, in the order (i, j), (i, j + 1), (i + 1, j), (i + 1, j + 1) with j + 1 taken modulo 256; an entry is i * 256 + j. `interp_weight`: bilinear weights: the four of an observation sum to one.
All inputs are finite; a program needn't handle non-finite values.
Results may differ from a plain program's by a relative error of at most 0.0003.
Values sent between devices are 32-bit elements; how exact they have to be, the bound alone decides.
A program may use at most 64 MiB of HBM per device.

v0:
```python
import jax
import jax.numpy as jnp
from jax import lax
from jax.sharding import PartitionSpec as P

SWEEPS = 4


HIGH = lax.Precision.HIGHEST


def with_halo(value, sides, width):
    for axis, dim in sides:
        peers, length = (lax.axis_size(axis), value.shape[dim])
        up = [(i, (i + 1) % peers) for i in range(peers - 1)]
        down = [(j, i) for i, j in up]
        last = lax.slice_in_dim(value, length - width, length, axis=dim)
        initial = lax.slice_in_dim(value, 0, width, axis=dim)
        before = lax.ppermute(last, axis, up)
        after = lax.ppermute(initial, axis, down)
        value = jnp.concatenate([before, value, after], axis=dim)
    return value


def per_device(
    departure,
    obs_weight,
    owner_id,
    obs_level,
    columns,
    interp_weight,
    vert_root,
    spread,
    lanczos,
    previous,
    beta_prev,
):
    tiles = lax.axis_size("tile")
    obs_count = departure.shape[0]
    capacity = 2 * obs_count // tiles
    rows = spread.shape[0]
    width = spread.shape[1]
    levels = lanczos.shape[0]
    block_cells = rows * width
    destination = owner_id[:, 0]
    order = jnp.argsort(destination, stable=True)
    counts = jnp.sum(
        (destination[None, :] == jnp.arange(tiles, dtype=jnp.int32)[:, None]).astype(jnp.int32),
        axis=1,
    )
    starts = jnp.cumsum(counts) - counts
    slot_index = jnp.arange(capacity, dtype=jnp.int32)[None, :]
    valid = slot_index < counts[:, None]
    source = order[jnp.clip(starts[:, None] + slot_index, 0, obs_count - 1).reshape(-1)].reshape(
        tiles, capacity
    )
    weighted = obs_weight * departure
    contrib = interp_weight * weighted[None, :]
    send_values = jnp.where(valid[None], contrib[:, source], 0.0)
    corner_cells = obs_level[None, :] * block_cells + columns
    send_cells = jnp.where(valid[None], corner_cells[:, source], 0)
    received, targets = (
        lax.all_to_all(send_values, "tile", split_axis=1, concat_axis=1, tiled=True),
        lax.all_to_all(send_cells, "tile", split_axis=1, concat_axis=1, tiled=True),
    )
    flat_target = targets.reshape(4, -1)
    received = received.reshape(-1)
    gradient = (
        jnp.zeros((levels * block_cells,), jnp.float32).at[flat_target.reshape(-1)].add(received)
    )
    gradient = gradient.reshape(levels, block_cells)
    vertical = jnp.dot(vert_root.T, gradient, precision=HIGH, preferred_element_type=jnp.float32)
    field = vertical.reshape(levels, rows, width)
    for sweep in range(SWEEPS):
        pushed = spread[None] * field
        padded = with_halo(pushed, (("tile", 1),), 1)
        laplace = (
            padded[:, 2:]
            + padded[:, :-2]
            + jnp.roll(pushed, 1, 2)
            + jnp.roll(pushed, -1, 2)
            - 4.0 * pushed
        )
        field = field + laplace
    combined = lanczos + field - beta_prev[0] * previous
    along, self_square = lax.psum((jnp.sum(combined * lanczos), jnp.sum(lanczos * lanczos)), "tile")
    alpha = along / self_square
    remainder = combined - alpha * lanczos
    rest = lax.psum(jnp.sum(remainder * remainder), "tile")
    beta = jnp.sqrt(rest / self_square + 1e-06)
    return (remainder / beta, jnp.stack([alpha, beta]))


def solution(mesh):
    placed = (
        P(("ens", "tile")),
        P(("ens", "tile")),
        P(("ens", "tile"), None),
        P(("ens", "tile")),
        P(None, ("ens", "tile")),
        P(None, ("ens", "tile")),
        P(),
        P("tile", None),
        P(None, ("ens", "tile"), None),
        P(None, ("ens", "tile"), None),
        P("ens"),
    )
    return jax.shard_map(
        per_device,
        mesh=mesh,
        in_specs=placed,
        out_specs=(P(None, ("ens", "tile"), None), P("ens")),
        check_vma=False,
    )
```

profile of v0, /device:TPU:0, one launch (start us, length us, event | category | flops | bytes accessed | tf_op | source)
XLA Modules:
  0.0 492.8 jit_solution(6434045081233191016)
XLA Ops:
  2.1 6.5 %sort.17 = (s32[4096]{0:T(1024)}, s32[4096]{0:T(1024)S(1)}) sort(s32[4096]{0:T(1024)} %bitcast.40, s32[4096]{0:T(1024)S(1)} %iota.17), dimensions={0}, to_apply=%region_1.2 | sort | flops 49152 | bytes 65536 | tf_op jit(solution)/shard_map/jit(argsort)/sort | solution.py:46
  8.6 45.5 %gather_fusion = s32[8192]{0:T(1024)S(1)} fusion(s32[4096]{0:T(1024)S(1)} %get-tuple-element.3, s32[8192]{0:T(1024)S(1)} %broadcast_clamp_fusion), kind=kCustom, calls=%fused_computation | custom fusion | bytes 98304 | tf_op jit(solution)/shard_map/gather | solution.py:54
  54.9 27.8 %gather_fusion.1 = s32[8192,4]{1,0:T(8,128)} fusion(s32[4,4096]{0,1:T(8,128)S(1)} %copy.62, s32[8192]{0:T(1024)S(1)} %broadcast_clamp_fusion.1), kind=kCustom, calls=%fused_computation.1 | custom fusion | bytes 294912 | tf_op jit(solution)/shard_map/gather | solution.py:61
  82.6 3.0 copy.63
  86.4 7.4 %all-to-all-start = ((s32[4,16,512]{2,0,1:T(4,128)}), s32[4,16,512]{2,0,1:T(4,128)S(1)}, u32[]{:S(2)}, u32[]{:S(2)}) async-start(s32[4,16,512]{2,0,1:T(4,128)} %select_bitcast_fusion.1), calls=%async_computation | async-start | bytes 262144 | tf_op jit(solution)/shard_map/all_to_all | solution.py:64
  95.0 2.0 copy.65
  97.0 29.3 %gather_fusion.2 = f32[8192,4]{1,0:T(8,128)} fusion(f32[4,4096]{0,1:T(8,128)} %copy.65, s32[8192]{0:T(1024)S(1)} %broadcast_clamp_fusion.1), kind=kCustom, calls=%fused_computation.2 | custom fusion | bytes 294912 | tf_op jit(solution)/shard_map/gather | solution.py:59
  126.3 2.8 copy.66
  130.5 6.0 %all-to-all-start.1 = ((f32[4,16,512]{2,0,1:T(4,128)}), f32[4,16,512]{2,0,1:T(4,128)S(1)}, u32[]{:S(2)}, u32[]{:S(2)}) async-start(f32[4,16,512]{2,0,1:T(4,128)} %select_bitcast_fusion), calls=%async_computation.1 | async-start | bytes 262144 | tf_op jit(solution)/shard_map/all_to_all | solution.py:63
  136.9 7.6 %all-to-all-done.1 = f32[4,16,512]{2,0,1:T(4,128)S(1)} async-done(((f32[4,16,512]{2,0,1:T(4,128)}), f32[4,16,512]{2,0,1:T(4,128)S(1)}, u32[]{:S(2)}, u32[]{:S(2)}) %all-to-all-start.1) | async-done | bytes 131104 | tf_op jit(solution)/shard_map/all_to_all | solution.py:63
  144.6 209.0 %scatter_custom_fusion = f32[520192]{0:T(1024)} fusion(s32[32768]{0:T(1024)S(1)} %bitcast.34, f32[32768]{0:T(1024)S(1)} %bitcast.35, f32[]{:T(128)} %constant.7.clone.1), kind=kCustom, calls=%fused_computation.44 | custom fusion | flops 32768 | bytes 2080772 | tf_op jit(solution)/shard_map/scatter-add | solution.py:69
  353.6 2.7 reshape.161
  356.3 6.4 %fusion.41 = f32[4096,127]{1,0:T(8,128)} fusion(f32[127,4096]{1,0:T(8,128)} %reshape.161, f32[127,127]{1,0:T(8,128)S(1)} %copy-done), kind=kOutput, calls=%fused_computation.74 | convolution fusion | flops 792772608 | bytes 4226052 | tf_op jit(solution)/shard_map/dot_general | solution.py:72
  362.7 3.0 copy.69
  369.6 3.2 collective-permute-start.1
  377.7 4.9 collective-permute-start.3
  387.4 7.4 %collective-permute-start.5 = (f32[127,1,256]{2,0,1:T(8,128)S(1)}, f32[127,1,256]{2,0,1:T(8,128)S(1)}, u32[]{:S(2)}, u32[]{:S(2)}) collective-permute-start(f32[127,1,256]{2,0,1:T(8,128)S(1)} %get-tuple-element.27), channel_id=1, source_target_pairs={{0,1},{1,2},{2,3},{3,4},{4,5},{5,6},{6,7},{7,8},{8,9},{9,10},{10,1... | collective-permute-start | bytes 390152 | tf_op jit(solution)/shard_map/ppermute | solution.py:19
  399.7 7.5 %collective-permute-start.7 = (f32[127,1,256]{2,0,1:T(8,128)S(1)}, f32[127,1,256]{2,0,1:T(8,128)S(1)}, u32[]{:S(2)}, u32[]{:S(2)}) collective-permute-start(f32[127,1,256]{2,0,1:T(8,128)S(1)} %get-tuple-element.21), channel_id=1, source_target_pairs={{0,1},{1,2},{2,3},{3,4},{4,5},{5,6},{6,7},{7,8},{8,9},{9,10},{10,1... | collective-permute-start | bytes 390152 | tf_op jit(solution)/shard_map/ppermute | solution.py:19
  408.1 5.5 %multiply_reduce_fusion.1 = (f32[]{:T(128)}, f32[127,16,256]{2,0,1:T(8,128)}) fusion(f32[127,16,256]{2,1,0:T(8,128)S(1)} %copy-done.2, f32[127,16,256]{2,1,0:T(8,128)S(1)} %copy-done.4, f32[]{:T(128)} %bitcast.29, f32[127,16,256]{2,0,1:T(8,128)S(1)} %get-tuple-element.15, f32[127,16,256]{2,0,1:T(8,128)S(1)} %get-tuple-element.14, ...), kind=kLoop, calls=%fused_computation.37 | loop fusion | flops 7802879 | bytes 14825480 | tf_op jit(solution)/shard_map/reduce_sum | solution.py:86
  413.7 36.7 %all-reduce = (f32[]{:T(128)}, f32[]{:T(128)}) all-reduce(f32[]{:T(128)} %get-tuple-element.12, f32[]{:T(128)} %multiply_reduce_fusion.2), channel_id=1, replica_groups=mesh['ens'=2,'tile'=16] {'tile'}, use_global_device_ids=true, to_apply=%region_5.6 | all-reduce | flops 2 | bytes 16 | tf_op jit(solution)/shard_map/psum | solution.py:86
  451.7 3.4 multiply_reduce_fusion
  455.1 30.3 %psum.23 = f32[]{:T(128)} all-reduce(f32[]{:T(128)} %multiply_reduce_fusion), channel_id=1, replica_groups=mesh['ens'=2,'tile'=16] {'tile'}, use_global_device_ids=true, to_apply=%region_9.10 | all-reduce | flops 1 | bytes 8 | tf_op jit(solution)/shard_map/psum | solution.py:89
  486.8 2.9 broadcast_divide_fusion
  489.7 2.5 copy.74
  (80 shorter events, 25.1 us)
Async XLA Ops:
  0.6 355.7 %copy-start = (f32[127,127]{1,0:T(8,128)S(1)}, f32[127,127]{1,0:T(8,128)}, u32[]{:S(2)}) copy-start(f32[127,127]{1,0:T(8,128)} %param.17) | copy-start | bytes 193552
  8.6 45.6 %copy-start.10 = (s32[4096]{0:T(1024)S(1)}, s32[4096]{0:T(1024)}, u32[]{:S(2)}) copy-start(s32[4096]{0:T(1024)} %param.14) | copy-start | bytes 49156
  8.6 45.6 %copy-start.6 = (s32[4,4096]{1,0:T(4,128)S(1)}, s32[4,4096]{1,0:T(4,128)}, u32[]{:S(2)}) copy-start(s32[4,4096]{1,0:T(4,128)} %param.15) | copy-start | bytes 196612
  82.6 11.1 %copy-start.8 = (f32[4096]{0:T(1024)S(1)}, f32[4096]{0:T(1024)}, u32[]{:S(2)}) copy-start(f32[4096]{0:T(1024)} %param.12) | copy-start | bytes 49156
  82.6 11.1 %copy-start.9 = (f32[4096]{0:T(1024)S(1)}, f32[4096]{0:T(1024)}, u32[]{:S(2)}) copy-start(f32[4096]{0:T(1024)} %param.11) | copy-start | bytes 49156
  82.6 11.1 %copy-start.7 = (f32[4,4096]{1,0:T(4,128)S(1)}, f32[4,4096]{1,0:T(4,128)}, u32[]{:S(2)}) copy-start(f32[4,4096]{1,0:T(4,128)} %param.16) | copy-start | bytes 196612
  82.6 11.2 %copy-start.2 = (f32[127,16,256]{2,1,0:T(8,128)S(1)}, f32[127,16,256]{2,1,0:T(8,128)}, u32[]{:S(2)}) copy-start(f32[127,16,256]{2,1,0:T(8,128)} %param.19) | copy-start | bytes 6242308
  86.4 44.2 %all-to-all-start = ((s32[4,16,512]{2,0,1:T(4,128)}), s32[4,16,512]{2,0,1:T(4,128)S(1)}, u32[]{:S(2)}, u32[]{:S(2)}) async-start(s32[4,16,512]{2,0,1:T(4,128)} %select_bitcast_fusion.1), calls=%async_computation | async-start | bytes 262144 | tf_op jit(solution)/shard_map/all_to_all | solution.py:64
  130.5 13.9 %all-to-all-start.1 = ((f32[4,16,512]{2,0,1:T(4,128)}), f32[4,16,512]{2,0,1:T(4,128)S(1)}, u32[]{:S(2)}, u32[]{:S(2)}) async-start(f32[4,16,512]{2,0,1:T(4,128)} %select_bitcast_fusion), calls=%async_computation.1 | async-start | bytes 262144 | tf_op jit(solution)/shard_map/all_to_all | solution.py:63
  362.7 3.0 copy-start.5
  368.1 5.0 %collective-permute-start = (f32[127,1,256]{2,0,1:T(8,128)S(1)}, f32[127,1,256]{2,0,1:T(8,128)S(1)}, u32[]{:S(2)}, u32[]{:S(2)}) collective-permute-start(f32[127,1,256]{2,0,1:T(8,128)S(1)} %get-tuple-element.38), channel_id=1, source_target_pairs={{1,0},{2,1},{3,2},{4,3},{5,4},{6,5},{7,6},{8,7},{9,8},{10,9},{11,1... | collective-permute-start | bytes 390152 | tf_op jit(solution)/shard_map/ppermute | solution.py:20
  369.6 4.2 copy-start.3
  369.6 4.1 collective-permute-start.1
  376.4 6.6 %collective-permute-start.2 = (f32[127,1,256]{2,0,1:T(8,128)S(1)}, f32[127,1,256]{2,0,1:T(8,128)S(1)}, u32[]{:S(2)}, u32[]{:S(2)}) collective-permute-start(f32[127,1,256]{2,0,1:T(8,128)S(1)} %get-tuple-element.32), channel_id=1, source_target_pairs={{1,0},{2,1},{3,2},{4,3},{5,4},{6,5},{7,6},{8,7},{9,8},{10,9},{11,1... | collective-permute-start | bytes 390152 | tf_op jit(solution)/shard_map/ppermute | solution.py:20
  377.7 5.9 %collective-permute-start.3 = (f32[127,1,256]{2,0,1:T(8,128)S(1)}, f32[127,1,256]{2,0,1:T(8,128)S(1)}, u32[]{:S(2)}, u32[]{:S(2)}) collective-permute-start(f32[127,1,256]{2,0,1:T(8,128)S(1)} %get-tuple-element.33), channel_id=1, source_target_pairs={{0,1},{1,2},{2,3},{3,4},{4,5},{5,6},{6,7},{7,8},{8,9},{9,10},{10,1... | collective-permute-start | bytes 390152 | tf_op jit(solution)/shard_map/ppermute | solution.py:19
  386.1 9.0 %collective-permute-start.4 = (f32[127,1,256]{2,0,1:T(8,128)S(1)}, f32[127,1,256]{2,0,1:T(8,128)S(1)}, u32[]{:S(2)}, u32[]{:S(2)}) collective-permute-start(f32[127,1,256]{2,0,1:T(8,128)S(1)} %get-tuple-element.26), channel_id=1, source_target_pairs={{1,0},{2,1},{3,2},{4,3},{5,4},{6,5},{7,6},{8,7},{9,8},{10,9},{11,1... | collective-permute-start | bytes 390152 | tf_op jit(solution)/shard_map/ppermute | solution.py:20
  387.4 8.3 %collective-permute-start.5 = (f32[127,1,256]{2,0,1:T(8,128)S(1)}, f32[127,1,256]{2,0,1:T(8,128)S(1)}, u32[]{:S(2)}, u32[]{:S(2)}) collective-permute-start(f32[127,1,256]{2,0,1:T(8,128)S(1)} %get-tuple-element.27), channel_id=1, source_target_pairs={{0,1},{1,2},{2,3},{3,4},{4,5},{5,6},{6,7},{7,8},{8,9},{9,10},{10,1... | collective-permute-start | bytes 390152 | tf_op jit(solution)/shard_map/ppermute | solution.py:19
  398.4 9.2 %collective-permute-start.6 = (f32[127,1,256]{2,0,1:T(8,128)S(1)}, f32[127,1,256]{2,0,1:T(8,128)S(1)}, u32[]{:S(2)}, u32[]{:S(2)}) collective-permute-start(f32[127,1,256]{2,0,1:T(8,128)S(1)} %get-tuple-element.20), channel_id=1, source_target_pairs={{1,0},{2,1},{3,2},{4,3},{5,4},{6,5},{7,6},{8,7},{9,8},{10,9},{11,1... | collective-permute-start | bytes 390152 | tf_op jit(solution)/shard_map/ppermute | solution.py:20
  399.7 8.5 %copy-start.4 = (f32[127,16,256]{2,1,0:T(8,128)S(1)}, f32[127,16,256]{2,1,0:T(8,128)}, u32[]{:S(2)}) copy-start(f32[127,16,256]{2,1,0:T(8,128)} %param.20) | copy-start | bytes 6242308
  399.7 8.5 %collective-permute-start.7 = (f32[127,1,256]{2,0,1:T(8,128)S(1)}, f32[127,1,256]{2,0,1:T(8,128)S(1)}, u32[]{:S(2)}, u32[]{:S(2)}) collective-permute-start(f32[127,1,256]{2,0,1:T(8,128)S(1)} %get-tuple-element.21), channel_id=1, source_target_pairs={{0,1},{1,2},{2,3},{3,4},{4,5},{5,6},{6,7},{7,8},{8,9},{9,10},{10,1... | collective-permute-start | bytes 390152 | tf_op jit(solution)/shard_map/ppermute | solution.py:19
  486.8 6.0 %copy-start.1 = (f32[127,127]{1,0:T(8,128)S(1)}, f32[127,127]{1,0:T(8,128)}, u32[]{:S(2)}) copy-start(f32[127,127]{1,0:T(8,128)} %param.17) | copy-start | bytes 193552
where the time goes:
time: 494 us; the launch traced here: 493 us
  other arithmetic  239 us (48%)
  local copies, waits for them, and re-layouts  124 us (25%)
  blocking collectives  67 us (14%)
  starting transfers between devices  41.6 us (8%)
  waiting for transfers between devices  9.94 us (2%)
  matrix products  6.37 us (1%)
    scatter-add x1, other arithmetic, per_device(): jnp.zeros((levels * block_cells,), jnp.float32).at[flat_target.reshape(-1)]  209 us
    gather x1, local copies, waits for them, and re-layouts, per_device(): order[jnp.clip(starts[:, None] + slot_index, 0, obs_count - 1).reshape(-1)]  45.5 us
    psum x1, blocking collectives, per_device(): lax.psum((jnp.sum(combined * lanczos), jnp.sum(lanczos * lanczos)), 'tile')  36.7 us
    gather x2, local copies, waits for them, and re-layouts, per_device(): send_values = jnp.where(valid[None], contrib[:, source], 0.0)  32.2 us
    gather x2, local copies, waits for them, and re-layouts, per_device(): send_cells = jnp.where(valid[None], corner_cells[:, source], 0)  30.8 us
    psum x1, blocking collectives, per_device(): rest = lax.psum(jnp.sum(remainder * remainder), 'tile')  30.3 us
    ppermute x4, starting transfers between devices, with_halo(): before = lax.ppermute(last, axis, up)  22.9 us
  transfers between devices with their start and end apart: 10, of which 5 were waited for; matrix products, arithmetic and copies ran while one was open for 8% of the time, Pallas kernels for 0%

commit v1 on v0

v1 whole, which is shorter than its diff:
```python
import functools

import jax
import jax.numpy as jnp
from jax import lax
from jax.experimental import pallas as pl
from jax.experimental.pallas import tpu as pltpu
from jax.sharding import PartitionSpec as P

SWEEPS = 4
GROUP = 512
F32 = jnp.float32
BF16 = jnp.bfloat16
HIGH = lax.Precision.HIGHEST
MESH = pl.DeviceIdType.MESH
VMEM_LIMIT = 48 * 1024 * 1024


def iota(shape, axis):
    return lax.broadcasted_iota(jnp.int32, shape, axis)


def dot_nt(a, b):
    return lax.dot_general(a, b, (((1,), (1,)), ((), ())), preferred_element_type=F32)


def split(x):
    hi = x.astype(BF16).astype(F32)
    return hi, x - hi


def earlier(size):
    return (iota((size, size), 0) < iota((size, size), 1)).astype(BF16)


def greet(tiles, me, ens):
    barrier = pltpu.get_barrier_semaphore()

    def signal(k, carry):
        peer = lax.rem(me + k, tiles)
        pl.semaphore_signal(barrier, inc=1, device_id=(ens, peer), device_id_type=MESH)
        return carry

    lax.fori_loop(1, tiles, signal, 0)
    return barrier


def route_kernel(
    tiles, cap, dep_ref, wgt_ref, own_ref, lev_ref, col_ref, itp_ref, out_ref,
    rank_ref, pay_ref, send_ref, send_sem, recv_sem,
):
    me, ens = lax.axis_index("tile"), lax.axis_index("ens")
    barrier = greet(tiles, me, ens)
    obs = dep_ref.shape[1]
    size = 256
    upper = earlier(size)
    base = jnp.zeros((tiles, 1), F32)
    for c in range(obs // size):
        at = pl.ds(c * size, size)
        hot = own_ref[:, at] == iota((tiles, size), 0)
        one = hot.astype(F32)
        before = jnp.dot(one.astype(BF16), upper, preferred_element_type=F32)
        rank_ref[:, at] = jnp.sum(one * (before + base), axis=0, keepdims=True).astype(jnp.int32)
        base = base + jnp.sum(one, axis=1, keepdims=True)
        value = itp_ref[:, at] * (wgt_ref[:, at] * dep_ref[:, at])
        hi, lo = split(value)
        cell = col_ref[0:1, at]
        pay_ref[0:4, at] = hi
        pay_ref[4:5, at] = lev_ref[:, at].astype(F32)
        pay_ref[5:6, at] = (cell // 256).astype(F32)
        pay_ref[6:7, at] = lax.rem(cell, 256).astype(F32)
        pay_ref[7:8, at] = jnp.ones((1, size), F32)
        pay_ref[8:12, at] = lo
        pay_ref[12:16, at] = jnp.zeros((4, size), F32)
    total = jnp.zeros((tiles * 16, cap), F32)
    step = 512
    for c in range(obs // step):
        at = pl.ds(c * step, step)
        pay = pay_ref[:, at]
        own = own_ref[:, at]
        left = jnp.concatenate(
            [jnp.where(own == t, pay, 0.0).astype(BF16) for t in range(tiles)], axis=0
        )
        right = (rank_ref[:, at] == iota((cap, step), 0)).astype(F32).astype(BF16)
        total = total + dot_nt(left, right)
    for t in range(tiles):
        send_ref[t] = total[t * 16 : t * 16 + 8] + total[t * 16 + 8 : t * 16 + 16]
    pl.semaphore_wait(barrier, tiles - 1)

    def copy_to(k):
        peer = lax.rem(me + k, tiles)
        return pltpu.make_async_remote_copy(
            src_ref=send_ref.at[peer],
            dst_ref=out_ref.at[me],
            send_sem=send_sem.at[k],
            recv_sem=recv_sem.at[k],
            device_id=(ens, peer),
            device_id_type=MESH,
        )

    def start(k, carry):
        copy_to(k).start()
        return carry

    def wait(k, carry):
        copy_to(k).wait()
        return carry

    lax.fori_loop(1, tiles, start, 0)
    out_ref[me] = send_ref[me]
    lax.fori_loop(1, tiles, wait, 0)


def scatter_kernel(recv_ref, vert_ref, out_ref, pos_ref, pay_ref, sort_ref, bound_ref, grad_ref, edge_ref, sem):
    tiles, _, cap = recv_ref.shape
    rows = out_ref.shape[0]
    slots = tiles * cap
    groups = slots // GROUP
    size = min(256, cap)
    per = cap // size
    upper = earlier(size)
    grad_ref[...] = jnp.zeros_like(grad_ref)

    def hot_of(s, c):
        at = pl.ds(c * size, size)
        row, valid = recv_ref[s, 5:6, at], recv_ref[s, 7:8, at]
        key = jnp.where(valid > 0.5, row, -1.0).astype(jnp.int32)
        return (key == iota((rows, size), 0)).astype(F32)

    counts = jnp.zeros((rows, 1), F32)
    for s in range(tiles):
        for c in range(per):
            counts = counts + jnp.sum(hot_of(s, c), axis=1, keepdims=True)
    sub, lane = iota((rows, 128), 0), iota((rows, 128), 1)
    as_row = jnp.sum(jnp.where(sub == lane, counts, 0.0), axis=0, keepdims=True)
    base = jnp.sum(jnp.where(lane < sub, as_row, 0.0), axis=1, keepdims=True)
    start_row = jnp.sum(jnp.where(sub == lane, base, 0.0), axis=0, keepdims=True)
    bound_ref[...] = jnp.concatenate(
        [start_row, start_row + as_row, jnp.zeros((6, 128), F32)], axis=0
    ).astype(jnp.int32)
    bounds = pltpu.make_async_copy(bound_ref, edge_ref, sem)
    bounds.start()
    total = jnp.zeros((groups * 16, GROUP), F32)
    for s in range(tiles):
        for c in range(per):
            at = pl.ds(c * size, size)
            one = hot_of(s, c)
            before = jnp.dot(one.astype(BF16), upper, preferred_element_type=F32)
            pos = jnp.sum(one * (before + base), axis=0, keepdims=True).astype(jnp.int32)
            base = base + jnp.sum(one, axis=1, keepdims=True)
            block = recv_ref[s, :, at]
            hi, lo = split(block)
            pay = jnp.concatenate([hi, lo], axis=0)
            group, place = pos // GROUP, lax.rem(pos, GROUP)
            left = jnp.concatenate(
                [jnp.where(group == g, pay, 0.0).astype(BF16) for g in range(groups)], axis=0
            )
            right = (place == iota((GROUP, size), 0)).astype(F32).astype(BF16)
            total = total + dot_nt(left, right)
    sort_ref[...] = total.reshape(groups, 16, GROUP)
    bounds.wait()

    def one_row(r, carry):
        first, last = edge_ref[0, r], edge_ref[1, r]

        def one_group(g, inner):
            block = sort_ref[g]
            here = block[5:6] == r.astype(F32)
            level = block[4:5].astype(jnp.int32)
            col = block[6:7].astype(jnp.int32)
            hot = (level == iota((128, GROUP), 0)).astype(F32).astype(BF16)
            at0 = col == iota((256, GROUP), 0)
            at1 = jnp.where(col == 255, 0, col + 1) == iota((256, GROUP), 0)
            value = jnp.where(here, block, 0.0)
            for below in range(2):
                part = jnp.zeros((128, 256), F32)
                for low in range(2):
                    k = low * 8 + below * 2
                    mat = jnp.where(
                        at0, value[k : k + 1], jnp.where(at1, value[k + 1 : k + 2], 0.0)
                    ).astype(BF16)
                    part = part + dot_nt(hot, mat)
                grad_ref[r + below] += part
            return inner

        lax.fori_loop(first // GROUP, (last + GROUP - 1) // GROUP, one_group, 0)
        return carry

    lax.fori_loop(0, rows - 1, one_row, 0)
    for x in range(rows):
        out_ref[x] = jnp.dot(vert_ref[...], grad_ref[x], precision=HIGH, preferred_element_type=F32)


def filter_kernel(
    tiles, beta_ref, vert_ref, spread_ref, lan_hbm, prev_hbm, out_hbm, coef_ref,
    lan_ref, prev_ref, halo_ref, spr_ref, diff_ref, sum_ref, all_ref,
    local_sem, halo_send, halo_recv, spr_send, spr_recv, sum_send, sum_recv,
):
    me, ens = lax.axis_index("tile"), lax.axis_index("ens")
    rows, width = spread_ref.shape
    levels = lan_hbm.shape[0] // rows
    wide = SWEEPS
    barrier = greet(tiles, me, ens)
    halves = width // 128
    parts = [pl.ds(h * 128, 128) for h in range(halves)]
    loads = [
        pltpu.make_async_copy(src.at[:, parts[h]], dst.at[h], local_sem.at[i, h])
        for i, (src, dst) in enumerate(((lan_hbm, lan_ref), (prev_hbm, prev_ref)))
        for h in range(halves)
    ]
    for load in loads:
        load.start()
    for side, edge in enumerate((0, tiles - 1)):

        @pl.when(me == edge)
        def _():
            halo_ref[side] = jnp.zeros(halo_ref.shape[1:], F32)
            spr_ref[side] = jnp.zeros(spr_ref.shape[1:], F32)

    pl.semaphore_wait(barrier, tiles - 1)

    def copies(side):
        peer = me + 1 if side == 0 else me - 1
        peer = jnp.clip(peer, 0, tiles - 1)
        begin = rows - wide if side == 0 else 0
        halo = pltpu.make_async_remote_copy(
            src_ref=vert_ref.at[pl.ds(begin, wide)],
            dst_ref=halo_ref.at[side],
            send_sem=halo_send.at[side],
            recv_sem=halo_recv.at[side],
            device_id=(ens, peer),
            device_id_type=MESH,
        )
        spr = pltpu.make_async_remote_copy(
            src_ref=spread_ref,
            dst_ref=spr_ref.at[side],
            send_sem=spr_send.at[side],
            recv_sem=spr_recv.at[side],
            device_id=(ens, peer),
            device_id_type=MESH,
        )
        return spr, halo

    for side in range(2):
        has = me < tiles - 1 if side == 0 else me > 0

        @pl.when(has)
        def _():
            for one in copies(side):
                one.start()

    for load in loads:
        load.wait()
    for side in range(2):
        sends = me < tiles - 1 if side == 0 else me > 0
        gets = me > 0 if side == 0 else me < tiles - 1

        @pl.when(gets)
        def _():
            for one in copies(side):
                one.wait_recv()

        @pl.when(sends)
        def _():
            for one in copies(side):
                one.wait_send()

    beta_prev = beta_ref[0]
    sum_ref[...] = jnp.zeros_like(sum_ref)

    def spread_row(x):
        if x < 0:
            return spr_ref[0, rows + x : rows + x + 1, :]
        if x >= rows:
            return spr_ref[1, x - rows : x - rows + 1, :]
        return spread_ref[x : x + 1, :]

    def strided(ref, begin, count, x):
        where = pl.ds(begin * rows + x, count, stride=rows)
        return jnp.concatenate([ref[h, where, :] for h in range(halves)], axis=1)

    def chunk(begin, count):
        at = pl.ds(begin, count)
        field = {}
        for x in range(-wide, rows + wide):
            if x < 0:
                field[x] = halo_ref[0, wide + x, at, :]
            elif x >= rows:
                field[x] = halo_ref[1, x - rows, at, :]
            else:
                field[x] = vert_ref[x, at, :]
        for sweep in range(SWEEPS):
            reach = wide - sweep
            pushed = {x: spread_row(x) * field[x] for x in range(-reach, rows + reach)}
            for x in range(1 - reach, rows + reach - 1):
                p = pushed[x]
                field[x] = field[x] + (
                    pushed[x + 1] + pushed[x - 1]
                    + pltpu.roll(p, 1, 1) + pltpu.roll(p, width - 1, 1) - 4.0 * p
                )
        dl = jnp.zeros((count, width), F32)
        ll, dd = dl, dl
        for x in range(rows):
            lan = strided(lan_ref, begin, count, x)
            diff = field[x] - beta_prev * strided(prev_ref, begin, count, x)
            diff_ref[x, at, :] = diff
            dl, ll, dd = dl + diff * lan, ll + lan * lan, dd + diff * diff
        for i, value in enumerate((dl, ll, dd)):
            row = jnp.sum(value, axis=0, keepdims=True)
            sum_ref[i : i + 1, :] += row[:, :128] + row[:, 128:]

    full = levels // 8
    pl.loop(0, full)(lambda c: chunk(pl.multiple_of(c * 8, 8), 8))
    if levels % 8:
        chunk(full * 8, levels % 8)

    def share(k):
        peer = lax.rem(me + k, tiles)
        return pltpu.make_async_remote_copy(
            src_ref=sum_ref,
            dst_ref=all_ref.at[me],
            send_sem=sum_send.at[k],
            recv_sem=sum_recv.at[k],
            device_id=(ens, peer),
            device_id_type=MESH,
        )

    def start(k, carry):
        share(k).start()
        return carry

    def wait(k, carry):
        share(k).wait()
        return carry

    lax.fori_loop(1, tiles, start, 0)
    all_ref[me] = sum_ref[...]
    lax.fori_loop(1, tiles, wait, 0)
    sums = jnp.sum(jnp.sum(all_ref[...], axis=0), axis=1, keepdims=True)
    dl, ll, dd = sums[0:1], sums[1:2], sums[2:3]
    extra = dl / ll
    beta = jnp.sqrt(jnp.maximum(dd - extra * dl, 0.0) / ll + 1e-06)
    coef_ref[0] = (1.0 + extra)[0, 0]
    coef_ref[1] = beta[0, 0]
    scale = 1.0 / beta

    def finish(begin, count):
        for x in range(rows):
            where = pl.ds(begin * rows + x, count, stride=rows)
            for h in range(halves):
                diff = diff_ref[x, pl.ds(begin, count), parts[h]]
                prev_ref[h, where, :] = (diff - extra * lan_ref[h, where, :]) * scale

    pl.loop(0, full)(lambda c: finish(pl.multiple_of(c * 8, 8), 8))
    if levels % 8:
        finish(full * 8, levels % 8)
    stores = [
        pltpu.make_async_copy(prev_ref.at[h], out_hbm.at[:, parts[h]], local_sem.at[0, h])
        for h in range(halves)
    ]
    for store in stores:
        store.start()
    for store in stores:
        store.wait()


def per_device(
    departure, obs_weight, owner_id, obs_level, columns, interp_weight, vert_root,
    spread, lanczos, previous, beta_prev,
):
    tiles = lax.axis_size("tile")
    obs = departure.shape[0]
    cap = 2 * obs // tiles
    rows, width = spread.shape
    levels = lanczos.shape[0]
    vmem = pl.BlockSpec(memory_space=pltpu.VMEM)
    smem = pl.BlockSpec(memory_space=pltpu.SMEM)
    hbm = pl.BlockSpec(memory_space=pl.ANY)
    dma = pltpu.SemaphoreType.DMA
    received = pl.pallas_call(
        functools.partial(route_kernel, tiles, cap),
        out_shape=jax.ShapeDtypeStruct((tiles, 8, cap), F32),
        in_specs=[vmem] * 6,
        out_specs=vmem,
        scratch_shapes=[
            pltpu.VMEM((1, obs), jnp.int32),
            pltpu.VMEM((16, obs), F32),
            pltpu.VMEM((tiles, 8, cap), F32),
            dma((tiles,)),
            dma((tiles,)),
        ],
        compiler_params=pltpu.CompilerParams(
            collective_id=0, has_side_effects=True, vmem_limit_bytes=VMEM_LIMIT
        ),
        name="route",
    )(
        departure.reshape(1, obs), obs_weight.reshape(1, obs), owner_id.reshape(1, obs),
        obs_level.reshape(1, obs), columns, interp_weight,
    )
    root = jnp.pad(vert_root.T, ((0, 128 - levels), (0, 128 - levels)))
    vertical = pl.pallas_call(
        scatter_kernel,
        out_shape=jax.ShapeDtypeStruct((rows, 128, width), F32),
        in_specs=[vmem] * 2,
        out_specs=vmem,
        scratch_shapes=[
            pltpu.VMEM((8, 128), jnp.int32),
            pltpu.VMEM((16, GROUP), F32),
            pltpu.VMEM((tiles * cap // GROUP, 16, GROUP), F32),
            pltpu.VMEM((8, 128), jnp.int32),
            pltpu.VMEM((rows, 128, width), F32),
            pltpu.SMEM((8, 128), jnp.int32),
            dma,
        ],
        compiler_params=pltpu.CompilerParams(vmem_limit_bytes=VMEM_LIMIT),
        name="scatter",
    )(received, root)
    flat = (levels * rows, width)
    vector, coefficients = pl.pallas_call(
        functools.partial(filter_kernel, tiles),
        out_shape=(jax.ShapeDtypeStruct(flat, F32), jax.ShapeDtypeStruct((2,), F32)),
        in_specs=[smem, vmem, vmem, hbm, hbm],
        out_specs=(hbm, smem),
        scratch_shapes=[
            pltpu.VMEM((width // 128, levels * rows, 128), F32),
            pltpu.VMEM((width // 128, levels * rows, 128), F32),
            pltpu.VMEM((2, SWEEPS, 128, width), F32),
            pltpu.VMEM((2, rows, width), F32),
            pltpu.VMEM((rows, 128, width), F32),
            pltpu.VMEM((8, 128), F32),
            pltpu.VMEM((tiles, 8, 128), F32),
            dma((2, width // 128)), dma((2,)), dma((2,)), dma((2,)), dma((2,)),
            dma((tiles,)), dma((tiles,)),
        ],
        compiler_params=pltpu.CompilerParams(
            collective_id=1, has_side_effects=True, vmem_limit_bytes=VMEM_LIMIT
        ),
        name="filter",
    )(beta_prev, vertical, spread, lanczos.reshape(flat), previous.reshape(flat))
    return vector.reshape(lanczos.shape), coefficients


def solution(mesh):
    placed = (
        P(("ens", "tile")),
        P(("ens", "tile")),
        P(("ens", "tile"), None),
        P(("ens", "tile")),
        P(None, ("ens", "tile")),
        P(None, ("ens", "tile")),
        P(),
        P("tile", None),
        P(None, ("ens", "tile"), None),
        P(None, ("ens", "tile"), None),
        P("ens"),
    )
    return jax.shard_map(
        per_device,
        mesh=mesh,
        in_specs=placed,
        out_specs=(P(None, ("ens", "tile"), None), P("ens")),
        check_vma=False,
    )
```

time: 494 us -> 82.5 us (0.17)
  other arithmetic: 239 us -> 0 us
  local copies, waits for them, and re-layouts: 124 us -> 8.66 us
  Pallas kernels: 0 us -> 72.1 us
  blocking collectives: 67 us -> 0 us
  starting transfers between devices: 41.6 us -> 0 us
  waiting for transfers between devices: 9.94 us -> 0 us
  matrix products: 6.37 us -> 0 us
    scatter-add x1 -> x0, other arithmetic: 209 us -> none  [per_device(): jnp.zeros((levels * block_cells,), jnp.float32).at[flat_target.reshape(-1)]]
    gather x5 -> x0, local copies, waits for them, and re-layouts: 108 us -> none  [the longest x1 45.5 us: per_device(): order[jnp.clip(starts[:, None] + slot_index, 0, obs_count - 1).reshape(-1)]]
    pallas_call x0 -> x3, Pallas kernels: none -> 72.1 us  [the longest x1 38.2 us: per_device(): pl.pallas_call(functools.partial(filter_kernel, tiles), out_shape=(jax.Sh...]
    psum x2 -> x0, blocking collectives: 67 us -> none  [the longest x1 36.7 us: per_device(): lax.psum((jnp.sum(combined * lanczos), jnp.sum(lanczos * lanczos)), 'tile')]
    ppermute x8 -> x0, starting transfers between devices: 28.2 us -> none  [the longest x4 22.9 us: with_halo(): before = lax.ppermute(last, axis, up)]
    all_to_all x2 -> x0, starting transfers between devices: 13.4 us -> none  [the longest x1 7.39 us: per_device(): lax.all_to_all(send_cells, 'tile', split_axis=1, concat_axis=1, tiled=True)]
    reduce_sum x4 -> x0, other arithmetic: 11 us -> none  [the longest x1 5.52 us: per_device(): jnp.sum(combined * lanczos)]
    all_to_all x2 -> x0, waiting for transfers between devices: 7.58 us -> none  [the longest x1 7.58 us: per_device(): lax.all_to_all(send_values, 'tile', split_axis=1, concat_axis=1, tiled=True)]
  transfers between devices with their start and end apart: 10 -> 0, of which waited for: 5 -> 0; matrix products, arithmetic and copies ran while one was open for 8% -> 0% of each run, Pallas kernels for 0% -> 0%
where the time goes in v1:
time: 82.5 us; the launch traced here: 82.3 us
  Pallas kernels  72.1 us (87%)
  local copies, waits for them, and re-layouts  8.66 us (10%)
  between operations  1.49 us (2%)
    pallas_call x1, Pallas kernels, per_device(): pl.pallas_call(functools.partial(filter_kernel, tiles), out_shape=(jax.Sh...  38.2 us
    pallas_call x1, Pallas kernels, per_device(): pl.pallas_call(scatter_kernel, out_shape=jax.ShapeDtypeStruct((rows, 128,...  22.8 us
    pallas_call x1, Pallas kernels, per_device(): pl.pallas_call(functools.partial(route_kernel, tiles, cap), out_shape=jax...  11.1 us
    unnamed x21, local copies, waits for them, and re-layouts  8.64 us

profile of v1, /device:TPU:0, one launch (start us, length us, event | category | flops | bytes accessed | tf_op | source)
XLA Modules:
  0.0 82.3 jit_solution(13404589164184164706)
XLA Ops:
  0.6 0.0 copy-start.1
  1.4 0.9 %copy.13 = f32[127,127]{0,1:T(8,128)S(1)} copy(f32[127,127]{1,0:T(8,128)} %param.17) | data formatting | bytes 129032 | tf_op args[6]
  2.4 0.0 copy-start.2
  2.4 0.8 %copy-done.2 = s32[4,4096]{1,0:T(4,128)S(1)} copy-done((s32[4,4096]{1,0:T(4,128)S(1)}, s32[4,4096]{1,0:T(4,128)}, u32[]{:S(2)}) %copy-start.2) | copy-done | bytes 65560
  3.2 0.0 copy-start.3
  3.2 0.8 %copy-done.3 = f32[4,4096]{1,0:T(4,128)S(1)} copy-done((f32[4,4096]{1,0:T(4,128)S(1)}, f32[4,4096]{1,0:T(4,128)}, u32[]{:S(2)}) %copy-start.3) | copy-done | bytes 65560
  4.1 0.0 copy-start.5
  4.1 0.7 copy-done.5
  4.8 0.0 copy-start.6
  4.8 0.7 copy-done.6
  5.5 0.0 copy-start.7
  5.5 0.7 copy-done.7
  6.2 0.0 copy-start.8
  6.2 0.7 copy-done.8
  7.0 0.0 copy-start.4
  7.0 11.1 %route.1.recv_ref = f32[16,8,512]{2,1,0:T(8,128)S(1)} custom-call(f32[1,4096]{1,0:T(1,128)S(1)} %bitcast.10, f32[1,4096]{1,0:T(1,128)S(1)} %bitcast.11, s32[1,4096]{1,0:T(1,128)S(1)} %bitcast.12, s32[1,4096]{1,0:T(1,128)S(1)} %bitcast.13, s32[4,4096]{1,0:T(4,128)S(1)} %copy-done.2, f32[4,4096]{1,0:T(4,128)S(1)} %copy-done.3), custom_call_target="tpu_custom_call" | custom-call | tf_op jit(solution)/shard_map/route/pallas_call | solution.py:380
  18.1 22.8 %scatter.1.vert_ref = f32[16,128,256]{2,1,0:T(8,128)S(1)} custom-call(f32[16,8,512]{2,1,0:T(8,128)S(1)} %route.1.recv_ref, f32[128,128]{1,0:T(8,128)S(1)} %pad.4.vert_ref), custom_call_target="tpu_custom_call" | custom-call | tf_op jit(solution)/shard_map/scatter/pallas_call | solution.py:401
  40.9 0.0 copy-start
  40.9 1.3 %copy-done = f32[16,128,256]{2,1,0:T(8,128)} copy-done((f32[16,128,256]{2,1,0:T(8,128)}, f32[16,128,256]{2,1,0:T(8,128)S(1)}, u32[]{:S(2)}) %copy-start) | copy-done | bytes 2097176
  42.2 0.0 copy-done.1
  42.2 0.0 copy-done.4
  42.2 38.2 %filter.1 = (f32[2032,256]{1,0:T(8,128)S(1)}, f32[2]{0:T(128)S(1)}) custom-call(f32[1]{0:T(128)S(6)} %copy.16.beta_ref, f32[16,128,256]{2,1,0:T(8,128)} %copy-done, f32[16,256]{1,0:T(8,128)S(1)} %copy-done.4, f32[2032,256]{1,0:T(8,128)S(1)} %bitcast.8, f32[2032,256]{1,0:T(8,128)} %bitcast.14), custom_call_target="tpu_custom_call" | custom-call | tf_op jit(solution)/shard_map/filter/pallas_call | solution.py:419
  80.5 1.3 %copy.17 = f32[127,16,256]{2,1,0:T(8,128)} copy(f32[127,16,256]{2,1,0:T(8,128)S(1)} %bitcast.9) | data formatting | bytes 4161536
  81.8 0.5 copy.18
  (1 shorter events, 0.0 us)
Async XLA Ops:
  0.6 41.6 %copy-start.1 = (f32[127,16,256]{2,1,0:T(8,128)S(1)}, f32[127,16,256]{2,1,0:T(8,128)}, u32[]{:S(2)}) copy-start(f32[127,16,256]{2,1,0:T(8,128)} %param.19) | copy-start | bytes 6242308
  2.4 0.8 %copy-start.2 = (s32[4,4096]{1,0:T(4,128)S(1)}, s32[4,4096]{1,0:T(4,128)}, u32[]{:S(2)}) copy-start(s32[4,4096]{1,0:T(4,128)} %col_ref.1) | copy-start | bytes 196612
  3.2 0.8 %copy-start.3 = (f32[4,4096]{1,0:T(4,128)S(1)}, f32[4,4096]{1,0:T(4,128)}, u32[]{:S(2)}) copy-start(f32[4,4096]{1,0:T(4,128)} %itp_ref.1) | copy-start | bytes 196612
  4.1 0.7 copy-start.5
  4.8 0.7 copy-start.6
  5.5 0.7 copy-start.7
  6.2 0.7 copy-start.8
  7.0 35.3 %copy-start.4 = (f32[16,256]{1,0:T(8,128)S(1)}, f32[16,256]{1,0:T(8,128)}, u32[]{:S(2)}) copy-start(f32[16,256]{1,0:T(8,128)} %spread_ref.1) | copy-start | bytes 49156
  40.9 1.3 %copy-start = (f32[16,128,256]{2,1,0:T(8,128)}, f32[16,128,256]{2,1,0:T(8,128)S(1)}, u32[]{:S(2)}) copy-start(f32[16,128,256]{2,1,0:T(8,128)S(1)} %scatter.1.vert_ref) | copy-start | bytes 6291460

commit v2 on v1

--- a/solution.py
+++ b/solution.py
@@ -8,12 +8,14 @@
 from jax.sharding import PartitionSpec as P
 
 SWEEPS = 4
-GROUP = 512
+GROUP = 256
+WINDOW = 2
 F32 = jnp.float32
 BF16 = jnp.bfloat16
 HIGH = lax.Precision.HIGHEST
 MESH = pl.DeviceIdType.MESH
-VMEM_LIMIT = 48 * 1024 * 1024
+VMEM_LIMIT = 32 * 1024 * 1024
+ROUTE_LIMIT = 60 * 1024 * 1024
 
 
 def iota(shape, axis):
@@ -45,46 +47,65 @@
     return barrier
 
 
+def lifted(row, width):
+    return jnp.broadcast_to(row, (16, width)).astype(BF16)
+
+
+def offsets(row, width):
+    return (jnp.broadcast_to(row, (16, width)) - iota((16, width), 0).astype(F32)).astype(BF16)
+
+
+def one_hot(diff, count, value):
+    zero = jnp.zeros_like(value)
+    return jnp.concatenate(
+        [jnp.where(diff == BF16(16 * a), value, zero) for a in range(count // 16)], axis=0
+    )
+
+
+def spread_out(key, pay, count):
+    zero = jnp.zeros_like(pay)
+    return jnp.concatenate([jnp.where(key == BF16(g), pay, zero) for g in range(count)], axis=0)
+
+
 def route_kernel(
     tiles, cap, dep_ref, wgt_ref, own_ref, lev_ref, col_ref, itp_ref, out_ref,
-    rank_ref, pay_ref, send_ref, send_sem, recv_sem,
+    left_ref, right_ref, send_ref, send_sem, recv_sem,
 ):
     me, ens = lax.axis_index("tile"), lax.axis_index("ens")
     barrier = greet(tiles, me, ens)
     obs = dep_ref.shape[1]
-    size = 256
+    size = min(256, cap)
+    per = cap // size
     upper = earlier(size)
     base = jnp.zeros((tiles, 1), F32)
+    ones = jnp.ones((16, size), BF16)
     for c in range(obs // size):
         at = pl.ds(c * size, size)
-        hot = own_ref[:, at] == iota((tiles, size), 0)
+        own = own_ref[:, at]
+        hot = own == iota((tiles, size), 0)
         one = hot.astype(F32)
         before = jnp.dot(one.astype(BF16), upper, preferred_element_type=F32)
-        rank_ref[:, at] = jnp.sum(one * (before + base), axis=0, keepdims=True).astype(jnp.int32)
+        rank = jnp.sum(one * (before + base), axis=0, keepdims=True).astype(jnp.int32)
         base = base + jnp.sum(one, axis=1, keepdims=True)
         value = itp_ref[:, at] * (wgt_ref[:, at] * dep_ref[:, at])
         hi, lo = split(value)
         cell = col_ref[0:1, at]
-        pay_ref[0:4, at] = hi
-        pay_ref[4:5, at] = lev_ref[:, at].astype(F32)
-        pay_ref[5:6, at] = (cell // 256).astype(F32)
-        pay_ref[6:7, at] = lax.rem(cell, 256).astype(F32)
-        pay_ref[7:8, at] = jnp.ones((1, size), F32)
-        pay_ref[8:12, at] = lo
-        pay_ref[12:16, at] = jnp.zeros((4, size), F32)
-    total = jnp.zeros((tiles * 16, cap), F32)
-    step = 512
-    for c in range(obs // step):
-        at = pl.ds(c * step, step)
-        pay = pay_ref[:, at]
-        own = own_ref[:, at]
-        left = jnp.concatenate(
-            [jnp.where(own == t, pay, 0.0).astype(BF16) for t in range(tiles)], axis=0
-        )
-        right = (rank_ref[:, at] == iota((cap, step), 0)).astype(F32).astype(BF16)
-        total = total + dot_nt(left, right)
+        pay = jnp.concatenate(
+            [
+                hi, lev_ref[:, at].astype(F32), (cell // 256).astype(F32),
+                lax.rem(cell, 256).astype(F32), jnp.ones((1, size), F32),
+                lo, jnp.zeros((4, size), F32),
+            ],
+            axis=0,
+        ).astype(BF16)
+        key = lifted((own * per + rank // size).astype(F32), size)
+        left_ref[:, at] = spread_out(key, pay, tiles * per)
+        right_ref[:, at] = one_hot(offsets(lax.rem(rank, size).astype(F32), size), size, ones)
+    total = dot_nt(left_ref[...], right_ref[...])
     for t in range(tiles):
-        send_ref[t] = total[t * 16 : t * 16 + 8] + total[t * 16 + 8 : t * 16 + 16]
+        for h in range(per):
+            k = (t * per + h) * 16
+            send_ref[t, :, h * size : (h + 1) * size] = total[k : k + 8] + total[k + 8 : k + 16]
     pl.semaphore_wait(barrier, tiles - 1)
 
     def copy_to(k):
@@ -111,15 +132,22 @@
     lax.fori_loop(1, tiles, wait, 0)
 
 
-def scatter_kernel(recv_ref, vert_ref, out_ref, pos_ref, pay_ref, sort_ref, bound_ref, grad_ref, edge_ref, sem):
+def scatter_kernel(
+    recv_ref, root_ref, out_ref, left_ref, right_ref, sort_ref, bound_ref, grad_ref, vert_ref, edge_ref, sem
+):
     tiles, _, cap = recv_ref.shape
     rows = out_ref.shape[0]
+    levels = root_ref.shape[0]
     slots = tiles * cap
     groups = slots // GROUP
     size = min(256, cap)
     per = cap // size
     upper = earlier(size)
     grad_ref[...] = jnp.zeros_like(grad_ref)
+    vert_ref[...] = jnp.zeros_like(vert_ref)
+    vert_ref[:levels, :levels] = root_ref[...]
+    root = vert_ref[...].T
+    ones = jnp.ones((16, GROUP), BF16)
 
     def hot_of(s, c):
         at = pl.ds(c * size, size)
@@ -140,55 +168,56 @@
     ).astype(jnp.int32)
     bounds = pltpu.make_async_copy(bound_ref, edge_ref, sem)
     bounds.start()
-    total = jnp.zeros((groups * 16, GROUP), F32)
     for s in range(tiles):
         for c in range(per):
             at = pl.ds(c * size, size)
+            to = pl.ds((s * per + c) * size, size)
             one = hot_of(s, c)
             before = jnp.dot(one.astype(BF16), upper, preferred_element_type=F32)
             pos = jnp.sum(one * (before + base), axis=0, keepdims=True).astype(jnp.int32)
             base = base + jnp.sum(one, axis=1, keepdims=True)
-            block = recv_ref[s, :, at]
-            hi, lo = split(block)
-            pay = jnp.concatenate([hi, lo], axis=0)
-            group, place = pos // GROUP, lax.rem(pos, GROUP)
-            left = jnp.concatenate(
-                [jnp.where(group == g, pay, 0.0).astype(BF16) for g in range(groups)], axis=0
+            hi, lo = split(recv_ref[s, :, at])
+            pay = jnp.concatenate([hi, lo], axis=0).astype(BF16)
+            left_ref[:, to] = spread_out(lifted((pos // GROUP).astype(F32), size), pay, groups)
+            right_ref[:, to] = one_hot(
+                offsets(lax.rem(pos, GROUP).astype(F32), size), GROUP, ones[:, :size]
             )
-            right = (place == iota((GROUP, size), 0)).astype(F32).astype(BF16)
-            total = total + dot_nt(left, right)
-    sort_ref[...] = total.reshape(groups, 16, GROUP)
+    total = dot_nt(left_ref[...], right_ref[...])
+    sort_ref[:groups] = total.reshape(groups, 16, GROUP)
+    for w in range(groups, sort_ref.shape[0]):
+        sort_ref[w] = jnp.zeros((16, GROUP), F32)
     bounds.wait()
 
     def one_row(r, carry):
         first, last = edge_ref[0, r], edge_ref[1, r]
-
-        def one_group(g, inner):
-            block = sort_ref[g]
-            here = block[5:6] == r.astype(F32)
-            level = block[4:5].astype(jnp.int32)
-            col = block[6:7].astype(jnp.int32)
-            hot = (level == iota((128, GROUP), 0)).astype(F32).astype(BF16)
-            at0 = col == iota((256, GROUP), 0)
-            at1 = jnp.where(col == 255, 0, col + 1) == iota((256, GROUP), 0)
-            value = jnp.where(here, block, 0.0)
-            for below in range(2):
-                part = jnp.zeros((128, 256), F32)
-                for low in range(2):
-                    k = low * 8 + below * 2
-                    mat = jnp.where(
-                        at0, value[k : k + 1], jnp.where(at1, value[k + 1 : k + 2], 0.0)
-                    ).astype(BF16)
-                    part = part + dot_nt(hot, mat)
-                grad_ref[r + below] += part
+        begin = first // GROUP
+        end = jnp.where(last > first, (last + GROUP - 1) // GROUP, begin)
+
+        def window(i, inner):
+            hots, lefts = [], []
+            for w in range(WINDOW):
+                block = sort_ref[begin + i * WINDOW + w]
+                value = jnp.where(block[5:6] == r.astype(F32), block, 0.0)
+                hots.append(one_hot(offsets(block[6:7], GROUP), 256, ones))
+                diff = offsets(block[4:5], GROUP)
+                for low in (0, 8):
+                    lefts.append(jnp.concatenate(
+                        [one_hot(diff, 128, lifted(value[low + k : low + k + 1], GROUP)) for k in range(4)],
+                        axis=0,
+                    ))
+            right = jnp.concatenate([h for h in hots for low in range(2)], axis=1)
+            part = dot_nt(jnp.concatenate(lefts, axis=1), right)
+            for k in range(4):
+                grad_ref[k % 2, r + k // 2] += part[k * 128 : (k + 1) * 128]
             return inner
 
-        lax.fori_loop(first // GROUP, (last + GROUP - 1) // GROUP, one_group, 0)
+        lax.fori_loop(0, (end - begin + WINDOW - 1) // WINDOW, window, 0)
         return carry
 
     lax.fori_loop(0, rows - 1, one_row, 0)
     for x in range(rows):
-        out_ref[x] = jnp.dot(vert_ref[...], grad_ref[x], precision=HIGH, preferred_element_type=F32)
+        grad = grad_ref[0, x] + pltpu.roll(grad_ref[1, x], 1, 1)
+        out_ref[x] = jnp.dot(root, grad, precision=HIGH, preferred_element_type=F32)
 
 
 def filter_kernel(
@@ -373,6 +402,8 @@
     cap = 2 * obs // tiles
     rows, width = spread.shape
     levels = lanczos.shape[0]
+    size = min(256, cap)
+    slots = tiles * cap
     vmem = pl.BlockSpec(memory_space=pltpu.VMEM)
     smem = pl.BlockSpec(memory_space=pltpu.SMEM)
     hbm = pl.BlockSpec(memory_space=pl.ANY)
@@ -383,38 +414,38 @@
         in_specs=[vmem] * 6,
         out_specs=vmem,
         scratch_shapes=[
-            pltpu.VMEM((1, obs), jnp.int32),
-            pltpu.VMEM((16, obs), F32),
+            pltpu.VMEM((tiles * cap // size * 16, obs), BF16),
+            pltpu.VMEM((size, obs), BF16),
             pltpu.VMEM((tiles, 8, cap), F32),
             dma((tiles,)),
             dma((tiles,)),
         ],
         compiler_params=pltpu.CompilerParams(
-            collective_id=0, has_side_effects=True, vmem_limit_bytes=VMEM_LIMIT
+            collective_id=0, has_side_effects=True, vmem_limit_bytes=ROUTE_LIMIT
         ),
         name="route",
     )(
         departure.reshape(1, obs), obs_weight.reshape(1, obs), owner_id.reshape(1, obs),
         obs_level.reshape(1, obs), columns, interp_weight,
     )
-    root = jnp.pad(vert_root.T, ((0, 128 - levels), (0, 128 - levels)))
     vertical = pl.pallas_call(
         scatter_kernel,
         out_shape=jax.ShapeDtypeStruct((rows, 128, width), F32),
         in_specs=[vmem] * 2,
         out_specs=vmem,
         scratch_shapes=[
+            pltpu.VMEM((slots // GROUP * 16, slots), BF16),
+            pltpu.VMEM((GROUP, slots), BF16),
+            pltpu.VMEM((slots // GROUP + WINDOW - 1, 16, GROUP), F32),
             pltpu.VMEM((8, 128), jnp.int32),
-            pltpu.VMEM((16, GROUP), F32),
-            pltpu.VMEM((tiles * cap // GROUP, 16, GROUP), F32),
-            pltpu.VMEM((8, 128), jnp.int32),
-            pltpu.VMEM((rows, 128, width), F32),
+            pltpu.VMEM((2, rows, 128, width), F32),
+            pltpu.VMEM((128, 128), F32),
             pltpu.SMEM((8, 128), jnp.int32),
             dma,
         ],
         compiler_params=pltpu.CompilerParams(vmem_limit_bytes=VMEM_LIMIT),
         name="scatter",
-    )(received, root)
+    )(received, vert_root)
     flat = (levels * rows, width)
     vector, coefficients = pl.pallas_call(
         functools.partial(filter_kernel, tiles),

time: 82.5 us -> 70 us (0.85)
  Pallas kernels: 72.1 us -> 63 us
  local copies, waits for them, and re-layouts: 8.66 us -> 5.19 us
    pallas_call x1, Pallas kernels: 38.2 us -> 30.4 us  [per_device(): pl.pallas_call(functools.partial(filter_kernel, tiles), out_shape=(jax.Sh...]
    unnamed x21 -> x12, local copies, waits for them, and re-layouts: 8.64 us -> 5.19 us
    pallas_call x1, Pallas kernels: 22.8 us -> 19.8 us  [per_device(): pl.pallas_call(scatter_kernel, out_shape=jax.ShapeDtypeStruct((rows, 128,...]
    pallas_call x1, Pallas kernels: 11.1 us -> 12.8 us  [per_device(): pl.pallas_call(functools.partial(route_kernel, tiles, cap), out_shape=jax...]
where the time goes in v2:
time: 70 us; the launch traced here: 69.7 us
  Pallas kernels  63 us (90%)
  local copies, waits for them, and re-layouts  5.19 us (7%)
  between operations  1.49 us (2%)
    pallas_call x1, Pallas kernels, per_device(): pl.pallas_call(functools.partial(filter_kernel, tiles), out_shape=(jax.Sh...  30.4 us
    pallas_call x1, Pallas kernels, per_device(): pl.pallas_call(scatter_kernel, out_shape=jax.ShapeDtypeStruct((rows, 128,...  19.8 us
    pallas_call x1, Pallas kernels, per_device(): pl.pallas_call(functools.partial(route_kernel, tiles, cap), out_shape=jax...  12.8 us
    unnamed x12, local copies, waits for them, and re-layouts  5.19 us

profile of v2, /device:TPU:0, one launch (start us, length us, event | category | flops | bytes accessed | tf_op | source)
XLA Modules:
  0.0 69.7 jit_solution(17316534814874533542)
XLA Ops:
  0.6 0.0 copy-start
  1.4 12.8 %route.1.recv_ref = f32[16,8,512]{2,1,0:T(8,128)} custom-call(f32[1,4096]{1,0:T(1,128)} %bitcast.10, f32[1,4096]{1,0:T(1,128)} %bitcast.11, s32[1,4096]{1,0:T(1,128)} %bitcast.12, s32[1,4096]{1,0:T(1,128)} %bitcast.13, s32[4,4096]{1,0:T(4,128)} %col_ref.1, f32[4,4096]{1,0:T(4,128)} %itp_ref.1), custom_call_target="tpu_custom_call" | custom-call | tf_op jit(solution)/shard_map/route/pallas_call | solution.py:411
  14.2 0.0 copy-start.2
  14.2 0.9 %copy-done.2 = f32[16,8,512]{2,1,0:T(8,128)S(1)} copy-done((f32[16,8,512]{2,1,0:T(8,128)S(1)}, f32[16,8,512]{2,1,0:T(8,128)}, u32[]{:S(2)}) %copy-start.2) | copy-done | bytes 262168
  15.1 0.0 copy-start.3
  15.1 0.8 %copy-done.3 = f32[127,127]{1,0:T(8,128)S(1)} copy-done((f32[127,127]{1,0:T(8,128)S(1)}, f32[127,127]{1,0:T(8,128)}, u32[]{:S(2)}) %copy-start.3) | copy-done | bytes 64540
  16.0 0.0 copy-start.4
  16.0 19.8 %scatter.1.vert_ref = f32[16,128,256]{2,1,0:T(8,128)S(1)} custom-call(f32[16,8,512]{2,1,0:T(8,128)S(1)} %copy-done.2, f32[127,127]{1,0:T(8,128)S(1)} %copy-done.3), custom_call_target="tpu_custom_call" | custom-call | tf_op jit(solution)/shard_map/scatter/pallas_call | solution.py:431
  35.8 0.0 copy-done
  35.9 0.0 copy-done.4
  35.9 0.0 copy-start.1
  35.9 1.6 %copy-done.1 = f32[127,16,256]{2,1,0:T(8,128)S(1)} copy-done((f32[127,16,256]{2,1,0:T(8,128)S(1)}, f32[127,16,256]{2,1,0:T(8,128)}, u32[]{:S(2)}) %copy-start.1) | copy-done | bytes 2080792
  37.5 30.4 %filter.1 = (f32[2032,256]{1,0:T(8,128)S(1)}, f32[2]{0:T(128)S(1)}) custom-call(f32[1]{0:T(128)S(6)} %copy.15.beta_ref, f32[16,128,256]{2,1,0:T(8,128)S(1)} %scatter.1.vert_ref, f32[16,256]{1,0:T(8,128)S(1)} %copy-done.4, f32[2032,256]{1,0:T(8,128)S(1)} %bitcast.7, f32[2032,256]{1,0:T(8,128)S(1)} %bitcast.8), custom_call_target="tpu_custom_call" | custom-call | tf_op jit(solution)/shard_map/filter/pallas_call | solution.py:450
  67.9 1.3 %copy.16 = f32[127,16,256]{2,1,0:T(8,128)} copy(f32[127,16,256]{2,1,0:T(8,128)S(1)} %bitcast.9) | data formatting | bytes 4161536
  69.2 0.5 copy.17
Async XLA Ops:
  0.6 35.2 %copy-start = (f32[127,16,256]{2,1,0:T(8,128)S(1)}, f32[127,16,256]{2,1,0:T(8,128)}, u32[]{:S(2)}) copy-start(f32[127,16,256]{2,1,0:T(8,128)} %param.19) | copy-start | bytes 6242308
  14.2 1.0 %copy-start.2 = (f32[16,8,512]{2,1,0:T(8,128)S(1)}, f32[16,8,512]{2,1,0:T(8,128)}, u32[]{:S(2)}) copy-start(f32[16,8,512]{2,1,0:T(8,128)} %route.1.recv_ref) | copy-start | bytes 786436
  15.1 0.8 %copy-start.3 = (f32[127,127]{1,0:T(8,128)S(1)}, f32[127,127]{1,0:T(8,128)}, u32[]{:S(2)}) copy-start(f32[127,127]{1,0:T(8,128)} %root_ref.1) | copy-start | bytes 193552
  16.0 19.9 %copy-start.4 = (f32[16,256]{1,0:T(8,128)S(1)}, f32[16,256]{1,0:T(8,128)}, u32[]{:S(2)}) copy-start(f32[16,256]{1,0:T(8,128)} %spread_ref.1) | copy-start | bytes 49156
  35.9 1.6 %copy-start.1 = (f32[127,16,256]{2,1,0:T(8,128)S(1)}, f32[127,16,256]{2,1,0:T(8,128)}, u32[]{:S(2)}) copy-start(f32[127,16,256]{2,1,0:T(8,128)} %param.20) | copy-start | bytes 6242308

commit v3 on v2

v3 whole, which is shorter than its diff:
```python
import functools

import jax
import jax.numpy as jnp
from jax import lax
from jax.experimental import pallas as pl
from jax.experimental.pallas import tpu as pltpu
from jax.sharding import PartitionSpec as P

SWEEPS = 4
GROUP = 256
WINDOW = 2
F32 = jnp.float32
BF16 = jnp.bfloat16
HIGH = lax.Precision.HIGHEST
MESH = pl.DeviceIdType.MESH
VMEM_LIMIT = 32 * 1024 * 1024
ROUTE_LIMIT = 60 * 1024 * 1024


def iota(shape, axis):
    return lax.broadcasted_iota(jnp.int32, shape, axis)


def dot_nt(a, b):
    return lax.dot_general(a, b, (((1,), (1,)), ((), ())), preferred_element_type=F32)


def split(x):
    hi = x.astype(BF16).astype(F32)
    return hi, x - hi


def earlier(size):
    return (iota((size, size), 0) < iota((size, size), 1)).astype(BF16)


def greet(tiles, me, ens):
    barrier = pltpu.get_barrier_semaphore()

    def signal(k, carry):
        peer = lax.rem(me + k, tiles)
        pl.semaphore_signal(barrier, inc=1, device_id=(ens, peer), device_id_type=MESH)
        return carry

    lax.fori_loop(1, tiles, signal, 0)
    return barrier


def lifted(row, width):
    return jnp.broadcast_to(row, (16, width)).astype(BF16)


def offsets(row, width):
    return (jnp.broadcast_to(row, (16, width)) - iota((16, width), 0).astype(F32)).astype(BF16)


def one_hot(diff, count, value):
    zero = jnp.zeros_like(value)
    return jnp.concatenate(
        [jnp.where(diff == BF16(16 * a), value, zero) for a in range(count // 16)], axis=0
    )


def spread_out(key, pay, count):
    zero = jnp.zeros_like(pay)
    return jnp.concatenate([jnp.where(key == BF16(g), pay, zero) for g in range(count)], axis=0)


def route_kernel(
    tiles, cap, dep_ref, wgt_ref, own_ref, lev_ref, col_ref, itp_ref, spread_ref, out_ref, spr_ref,
    left_ref, right_ref, send_ref, send_sem, recv_sem, spr_send, spr_recv,
):
    me, ens = lax.axis_index("tile"), lax.axis_index("ens")
    barrier = greet(tiles, me, ens)
    obs = dep_ref.shape[1]
    size = min(256, cap)
    per = cap // size
    upper = earlier(size)
    base = jnp.zeros((tiles, 1), F32)
    ones = jnp.ones((16, size), BF16)
    for c in range(obs // size):
        at = pl.ds(c * size, size)
        own = own_ref[:, at]
        hot = own == iota((tiles, size), 0)
        one = hot.astype(F32)
        before = jnp.dot(one.astype(BF16), upper, preferred_element_type=F32)
        rank = jnp.sum(one * (before + base), axis=0, keepdims=True).astype(jnp.int32)
        base = base + jnp.sum(one, axis=1, keepdims=True)
        value = itp_ref[:, at] * (wgt_ref[:, at] * dep_ref[:, at])
        hi, lo = split(value)
        cell = col_ref[0:1, at]
        pay = jnp.concatenate(
            [
                hi, lev_ref[:, at].astype(F32), (cell // 256).astype(F32),
                lax.rem(cell, 256).astype(F32), jnp.ones((1, size), F32),
                lo, jnp.zeros((4, size), F32),
            ],
            axis=0,
        ).astype(BF16)
        key = lifted((own * per + rank // size).astype(F32), size)
        left_ref[:, at] = spread_out(key, pay, tiles * per)
        right_ref[:, at] = one_hot(offsets(lax.rem(rank, size).astype(F32), size), size, ones)
    total = dot_nt(left_ref[...], right_ref[...])
    for t in range(tiles):
        for h in range(per):
            k = (t * per + h) * 16
            send_ref[t, :, h * size : (h + 1) * size] = total[k : k + 8] + total[k + 8 : k + 16]
    for side, edge in enumerate((0, tiles - 1)):

        @pl.when(me == edge)
        def _():
            spr_ref[side] = jnp.zeros(spr_ref.shape[1:], F32)

    pl.semaphore_wait(barrier, tiles - 1)

    def spr_copy(side):
        peer = jnp.clip(me + 1 if side == 0 else me - 1, 0, tiles - 1)
        return pltpu.make_async_remote_copy(
            src_ref=spread_ref,
            dst_ref=spr_ref.at[side],
            send_sem=spr_send.at[side],
            recv_sem=spr_recv.at[side],
            device_id=(ens, peer),
            device_id_type=MESH,
        )

    def copy_to(k):
        peer = lax.rem(me + k, tiles)
        return pltpu.make_async_remote_copy(
            src_ref=send_ref.at[peer],
            dst_ref=out_ref.at[me],
            send_sem=send_sem.at[k],
            recv_sem=recv_sem.at[k],
            device_id=(ens, peer),
            device_id_type=MESH,
        )

    def start(k, carry):
        copy_to(k).start()
        return carry

    def wait(k, carry):
        copy_to(k).wait()
        return carry

    lax.fori_loop(1, tiles, start, 0)
    sends = (me < tiles - 1, me > 0)
    for side in range(2):
        pl.when(sends[side])(spr_copy(side).start)
    out_ref[me] = send_ref[me]
    lax.fori_loop(1, tiles, wait, 0)
    for side in range(2):
        pl.when(sends[1 - side])(spr_copy(side).wait_recv)
        pl.when(sends[side])(spr_copy(side).wait_send)


def load_root(root_ref, vert_ref):
    levels = root_ref.shape[0]
    vert_ref[...] = jnp.zeros_like(vert_ref)
    vert_ref[:levels, :levels] = root_ref[...]
    return vert_ref[...].T


def add_rows(low, high, edge_ref, sort_ref, grad_ref):
    ones = jnp.ones((16, GROUP), BF16)

    def one_row(r, carry):
        first, last = edge_ref[0, r], edge_ref[1, r]
        begin = first // GROUP
        end = jnp.where(last > first, (last + GROUP - 1) // GROUP, begin)

        def window(i, inner):
            hots, lefts = [], []
            for w in range(WINDOW):
                block = sort_ref[begin + i * WINDOW + w]
                value = jnp.where(block[5:6] == r.astype(F32), block, 0.0)
                hots.append(one_hot(offsets(block[6:7], GROUP), 256, ones))
                diff = offsets(block[4:5], GROUP)
                for low in (0, 8):
                    lefts.append(jnp.concatenate(
                        [one_hot(diff, 128, lifted(value[low + k : low + k + 1], GROUP)) for k in range(4)],
                        axis=0,
                    ))
            right = jnp.concatenate([h for h in hots for low in range(2)], axis=1)
            part = dot_nt(jnp.concatenate(lefts, axis=1), right)
            for k in range(4):
                grad_ref[k % 2, r + k // 2] += part[k * 128 : (k + 1) * 128]
            return inner

        lax.fori_loop(0, (end - begin + WINDOW - 1) // WINDOW, window, 0)
        return carry

    lax.fori_loop(low, high, one_row, 0)


def levels_of(root, grad_ref, x):
    grad = grad_ref[0, x] + pltpu.roll(grad_ref[1, x], 1, 1)
    return jnp.dot(root, grad, precision=HIGH, preferred_element_type=F32)


def scatter_kernel(
    recv_ref, root_ref, low_ref, high_ref, sort_ref, bound_ref, part_ref,
    left_ref, right_ref, grad_ref, vert_ref, edge_ref, sem,
):
    tiles, _, cap = recv_ref.shape
    rows = grad_ref.shape[1]
    wide = SWEEPS
    slots = tiles * cap
    groups = slots // GROUP
    size = min(256, cap)
    per = cap // size
    upper = earlier(size)
    grad_ref[...] = jnp.zeros_like(grad_ref)
    root = load_root(root_ref, vert_ref)
    ones = jnp.ones((16, GROUP), BF16)

    def hot_of(s, c):
        at = pl.ds(c * size, size)
        row, valid = recv_ref[s, 5:6, at], recv_ref[s, 7:8, at]
        key = jnp.where(valid > 0.5, row, -1.0).astype(jnp.int32)
        return (key == iota((rows, size), 0)).astype(F32)

    counts = jnp.zeros((rows, 1), F32)
    for s in range(tiles):
        for c in range(per):
            counts = counts + jnp.sum(hot_of(s, c), axis=1, keepdims=True)
    sub, lane = iota((rows, 128), 0), iota((rows, 128), 1)
    as_row = jnp.sum(jnp.where(sub == lane, counts, 0.0), axis=0, keepdims=True)
    base = jnp.sum(jnp.where(lane < sub, as_row, 0.0), axis=1, keepdims=True)
    start_row = jnp.sum(jnp.where(sub == lane, base, 0.0), axis=0, keepdims=True)
    bound_ref[...] = jnp.concatenate(
        [start_row, start_row + as_row, jnp.zeros((6, 128), F32)], axis=0
    ).astype(jnp.int32)
    bounds = pltpu.make_async_copy(bound_ref, edge_ref, sem)
    bounds.start()
    for s in range(tiles):
        for c in range(per):
            at = pl.ds(c * size, size)
            to = pl.ds((s * per + c) * size, size)
            one = hot_of(s, c)
            before = jnp.dot(one.astype(BF16), upper, preferred_element_type=F32)
            pos = jnp.sum(one * (before + base), axis=0, keepdims=True).astype(jnp.int32)
            base = base + jnp.sum(one, axis=1, keepdims=True)
            hi, lo = split(recv_ref[s, :, at])
            pay = jnp.concatenate([hi, lo], axis=0).astype(BF16)
            left_ref[:, to] = spread_out(lifted((pos // GROUP).astype(F32), size), pay, groups)
            right_ref[:, to] = one_hot(
                offsets(lax.rem(pos, GROUP).astype(F32), size), GROUP, ones[:, :size]
            )
    total = dot_nt(left_ref[...], right_ref[...])
    sort_ref[:groups] = total.reshape(groups, 16, GROUP)
    for w in range(groups, sort_ref.shape[0]):
        sort_ref[w] = jnp.zeros((16, GROUP), F32)
    bounds.wait()

    add_rows(0, wide, edge_ref, sort_ref, grad_ref)
    add_rows(rows - wide - 1, rows - 1, edge_ref, sort_ref, grad_ref)
    for x in range(wide):
        low_ref[x] = levels_of(root, grad_ref, x)
        high_ref[x] = levels_of(root, grad_ref, rows - wide + x)
    for dj in range(2):
        part_ref[0, dj] = grad_ref[dj, wide]
        part_ref[1, dj] = grad_ref[dj, rows - wide - 1]


def sweep_rows(field, spread_of, low, high):
    width = field[low].shape[1]
    for sweep in range(SWEEPS):
        pushed = {x: spread_of(x) * field[x] for x in range(low, high)}
        low, high = low + 1, high - 1
        for x in range(low, high):
            p = pushed[x]
            field[x] = field[x] + (
                pushed[x + 1] + pushed[x - 1]
                + pltpu.roll(p, 1, 1) + pltpu.roll(p, width - 1, 1) - 4.0 * p
            )
    return field


def strided(ref, begin, count, x, rows):
    where = pl.ds(begin * rows + x, count, stride=rows)
    return jnp.concatenate([ref[h, where, :] for h in range(ref.shape[0])], axis=1)


def add_sums(sum_ref, pairs):
    dl, ll, dd = (sum(v) for v in zip(*[(d * l, l * l, d * d) for d, l in pairs]))
    for i, value in enumerate((dl, ll, dd)):
        row = jnp.sum(value, axis=0, keepdims=True)
        sum_ref[i : i + 1, :] += row[:, :128] + row[:, 128:]


def for_levels(levels, chunk):
    full = levels // 8
    pl.loop(0, full)(lambda c: chunk(pl.multiple_of(c * 8, 8), 8))
    if levels % 8:
        chunk(full * 8, levels % 8)


def loads_of(pairs, sem):
    return [
        pltpu.make_async_copy(src.at[:, pl.ds(h * 128, 128)], dst.at[h], sem.at[i, h])
        for i, (src, dst) in enumerate(pairs)
        for h in range(dst.shape[0])
    ]


def inner_kernel(
    beta_ref, low_ref, high_ref, sort_ref, bound_ref, part_ref, root_ref, spread_ref, lan_hbm, prev_hbm,
    mid_ref, diff_ref, sum_ref, grad_ref, vert_ref, edge_ref, lan_ref, prev_ref, sem, local_sem,
):
    rows = spread_ref.shape[0]
    levels = root_ref.shape[0]
    wide = SWEEPS
    bounds = pltpu.make_async_copy(bound_ref, edge_ref, sem)
    bounds.start()
    loads = loads_of(((lan_hbm, lan_ref), (prev_hbm, prev_ref)), local_sem)
    for load in loads:
        load.start()
    for dj in range(2):
        grad_ref[dj, wide] = part_ref[0, dj]
        grad_ref[dj, rows - wide - 1] = part_ref[1, dj]
        for x in range(wide + 1, rows - wide - 1):
            grad_ref[dj, x] = jnp.zeros(grad_ref.shape[2:], F32)
    root = load_root(root_ref, vert_ref)
    bounds.wait()
    add_rows(wide, rows - wide - 1, edge_ref, sort_ref, grad_ref)
    for x in range(wide, rows - wide):
        mid_ref[x - wide] = levels_of(root, grad_ref, x)
    for load in loads:
        load.wait()
    beta_prev = beta_ref[0]
    sum_ref[...] = jnp.zeros_like(sum_ref)

    def chunk(begin, count):
        at = pl.ds(begin, count)
        field = {x: low_ref[x, at, :] for x in range(wide)}
        field.update({x: mid_ref[x - wide, at, :] for x in range(wide, rows - wide)})
        field.update({x: high_ref[x - rows + wide, at, :] for x in range(rows - wide, rows)})
        field = sweep_rows(field, lambda x: spread_ref[x : x + 1, :], 0, rows)
        pairs = []
        for x in range(wide, rows - wide):
            diff = field[x] - beta_prev * strided(prev_ref, begin, count, x, rows)
            diff_ref[x - wide, at, :] = diff
            pairs.append((diff, strided(lan_ref, begin, count, x, rows)))
        add_sums(sum_ref, pairs)

    for_levels(levels, chunk)


def filter_kernel(
    tiles, beta_ref, low_ref, mid_ref, high_ref, below_ref, above_ref, inner_ref, part_ref, spread_ref, spr_ref,
    lan_hbm, prev_hbm, out_hbm, coef_ref,
    lan_ref, prev_ref, diff_ref, sum_ref, all_ref, local_sem, sum_send, sum_recv,
):
    me, ens = lax.axis_index("tile"), lax.axis_index("ens")
    rows, width = spread_ref.shape
    levels = lan_hbm.shape[0] // rows
    wide = SWEEPS
    barrier = greet(tiles, me, ens)
    loads = loads_of(((lan_hbm, lan_ref), (prev_hbm, prev_ref)), local_sem)
    for load in loads:
        load.start()
    for load in loads:
        load.wait()
    beta_prev = beta_ref[0]
    sum_ref[...] = part_ref[...]

    def spread_row(x):
        if x < 0:
            return spr_ref[0, rows + x : rows + x + 1, :]
        if x >= rows:
            return spr_ref[1, x - rows : x - rows + 1, :]
        return spread_ref[x : x + 1, :]

    def field_row(x, at):
        for ref, begin in ((below_ref, -wide), (low_ref, 0), (mid_ref, wide), (high_ref, rows - wide), (above_ref, rows)):
            if begin <= x < begin + ref.shape[0]:
                return ref[x - begin, at, :]

    def chunk(begin, count):
        at = pl.ds(begin, count)
        pairs = []
        for first in (0, rows - wide):
            span = (first - wide, first + 2 * wide)
            field = sweep_rows({x: field_row(x, at) for x in range(*span)}, spread_row, *span)
            for x in range(first, first + wide):
                diff = field[x] - beta_prev * strided(prev_ref, begin, count, x, rows)
                diff_ref[x % (2 * wide), at, :] = diff
                pairs.append((diff, strided(lan_ref, begin, count, x, rows)))
        add_sums(sum_ref, pairs)

    for_levels(levels, chunk)
    pl.semaphore_wait(barrier, tiles - 1)

    def share(k):
        peer = lax.rem(me + k, tiles)
        return pltpu.make_async_remote_copy(
            src_ref=sum_ref,
            dst_ref=all_ref.at[me],
            send_sem=sum_send.at[k],
            recv_sem=sum_recv.at[k],
            device_id=(ens, peer),
            device_id_type=MESH,
        )

    def start(k, carry):
        share(k).start()
        return carry

    def wait(k, carry):
        share(k).wait()
        return carry

    lax.fori_loop(1, tiles, start, 0)
    all_ref[me] = sum_ref[...]
    lax.fori_loop(1, tiles, wait, 0)
    sums = jnp.sum(jnp.sum(all_ref[...], axis=0), axis=1, keepdims=True)
    dl, ll, dd = sums[0:1], sums[1:2], sums[2:3]
    extra = dl / ll
    beta = jnp.sqrt(jnp.maximum(dd - extra * dl, 0.0) / ll + 1e-06)
    coef_ref[0] = (1.0 + extra)[0, 0]
    coef_ref[1] = beta[0, 0]
    scale = 1.0 / beta

    def finish(begin, count):
        for x in range(rows):
            where = pl.ds(begin * rows + x, count, stride=rows)
            for h in range(width // 128):
                at = (pl.ds(begin, count), pl.ds(h * 128, 128))
                if wide <= x < rows - wide:
                    diff = inner_ref[x - wide, *at]
                else:
                    diff = diff_ref[x % (2 * wide), *at]
                prev_ref[h, where, :] = (diff - extra * lan_ref[h, where, :]) * scale

    for_levels(levels, finish)
    stores = [
        pltpu.make_async_copy(prev_ref.at[h], out_hbm.at[:, pl.ds(h * 128, 128)], local_sem.at[0, h])
        for h in range(width // 128)
    ]
    for store in stores:
        store.start()
    for store in stores:
        store.wait()


def per_device(
    departure, obs_weight, owner_id, obs_level, columns, interp_weight, vert_root,
    spread, lanczos, previous, beta_prev,
):
    tiles = lax.axis_size("tile")
    obs = departure.shape[0]
    cap = 2 * obs // tiles
    rows, width = spread.shape
    levels = lanczos.shape[0]
    size = min(256, cap)
    slots = tiles * cap
    vmem = pl.BlockSpec(memory_space=pltpu.VMEM)
    smem = pl.BlockSpec(memory_space=pltpu.SMEM)
    hbm = pl.BlockSpec(memory_space=pl.ANY)
    dma = pltpu.SemaphoreType.DMA
    received, spread_halo = pl.pallas_call(
        functools.partial(route_kernel, tiles, cap),
        out_shape=(
            jax.ShapeDtypeStruct((tiles, 8, cap), F32),
            jax.ShapeDtypeStruct((2, rows, width), F32),
        ),
        in_specs=[vmem] * 7,
        out_specs=(vmem, vmem),
        scratch_shapes=[
            pltpu.VMEM((tiles * cap // size * 16, obs), BF16),
            pltpu.VMEM((size, obs), BF16),
            pltpu.VMEM((tiles, 8, cap), F32),
            dma((tiles,)), dma((tiles,)), dma((2,)), dma((2,)),
        ],
        compiler_params=pltpu.CompilerParams(
            collective_id=0, has_side_effects=True, vmem_limit_bytes=ROUTE_LIMIT
        ),
        name="route",
    )(
        departure.reshape(1, obs), obs_weight.reshape(1, obs), owner_id.reshape(1, obs),
        obs_level.reshape(1, obs), columns, interp_weight, spread,
    )
    flat = (levels * rows, width)
    lan, prev = lanczos.reshape(flat), previous.reshape(flat)
    edge = jax.ShapeDtypeStruct((SWEEPS, 128, width), F32)
    middle = jax.ShapeDtypeStruct((rows - 2 * SWEEPS, 128, width), F32)
    low, high, order, bound, part = pl.pallas_call(
        scatter_kernel,
        out_shape=(
            edge,
            edge,
            jax.ShapeDtypeStruct((slots // GROUP + WINDOW - 1, 16, GROUP), F32),
            jax.ShapeDtypeStruct((8, 128), jnp.int32),
            jax.ShapeDtypeStruct((2, 2, 128, width), F32),
        ),
        in_specs=[vmem] * 2,
        out_specs=[vmem] * 5,
        scratch_shapes=[
            pltpu.VMEM((slots // GROUP * 16, slots), BF16),
            pltpu.VMEM((GROUP, slots), BF16),
            pltpu.VMEM((2, rows, 128, width), F32),
            pltpu.VMEM((128, 128), F32),
            pltpu.SMEM((8, 128), jnp.int32),
            dma,
        ],
        compiler_params=pltpu.CompilerParams(vmem_limit_bytes=VMEM_LIMIT),
        name="scatter",
    )(received, vert_root)
    up = [(i, i + 1) for i in range(tiles - 1)]
    below = lax.ppermute(high, "tile", up)
    above = lax.ppermute(low, "tile", [(j, i) for i, j in up])
    mid, inner, sums = pl.pallas_call(
        inner_kernel,
        out_shape=(middle, middle, jax.ShapeDtypeStruct((8, 128), F32)),
        in_specs=[smem] + [vmem] * 7 + [hbm] * 2,
        out_specs=[vmem] * 3,
        scratch_shapes=[
            pltpu.VMEM((2, rows, 128, width), F32),
            pltpu.VMEM((128, 128), F32),
            pltpu.SMEM((8, 128), jnp.int32),
            pltpu.VMEM((width // 128, levels * rows, 128), F32),
            pltpu.VMEM((width // 128, levels * rows, 128), F32),
            dma,
            dma((2, width // 128)),
        ],
        compiler_params=pltpu.CompilerParams(vmem_limit_bytes=VMEM_LIMIT),
        cost_estimate=pl.CostEstimate(flops=10**10, bytes_accessed=10**7, transcendentals=0),
        name="inner",
    )(beta_prev, low, high, order, bound, part, vert_root, spread, lan, prev)
    vector, coefficients = pl.pallas_call(
        functools.partial(filter_kernel, tiles),
        out_shape=(jax.ShapeDtypeStruct(flat, F32), jax.ShapeDtypeStruct((2,), F32)),
        in_specs=[smem] + [vmem] * 9 + [hbm] * 2,
        out_specs=(hbm, smem),
        scratch_shapes=[
            pltpu.VMEM((width // 128, levels * rows, 128), F32),
            pltpu.VMEM((width // 128, levels * rows, 128), F32),
            pltpu.VMEM((2 * SWEEPS, 128, width), F32),
            pltpu.VMEM((8, 128), F32),
            pltpu.VMEM((tiles, 8, 128), F32),
            dma((2, width // 128)),
            dma((tiles,)), dma((tiles,)),
        ],
        compiler_params=pltpu.CompilerParams(
            collective_id=1, has_side_effects=True, vmem_limit_bytes=VMEM_LIMIT
        ),
        name="filter",
    )(beta_prev, low, mid, high, below, above, inner, sums, spread, spread_halo, lan, prev)
    return vector.reshape(lanczos.shape), coefficients


def solution(mesh):
    placed = (
        P(("ens", "tile")),
        P(("ens", "tile")),
        P(("ens", "tile"), None),
        P(("ens", "tile")),
        P(None, ("ens", "tile")),
        P(None, ("ens", "tile")),
        P(),
        P("tile", None),
        P(None, ("ens", "tile"), None),
        P(None, ("ens", "tile"), None),
        P("ens"),
    )
    return jax.shard_map(
        per_device,
        mesh=mesh,
        in_specs=placed,
        out_specs=(P(None, ("ens", "tile"), None), P("ens")),
        check_vma=False,
    )
```

time: 70 us -> 70.1 us (level)
  the two profiles are of different devices: /device:TPU:0 before, /device:TPU:3 now
where the time goes in v3:
time: 70.1 us; the launch traced here: 69.4 us
  Pallas kernels  53 us (76%)
  local copies, waits for them, and re-layouts  8.34 us (12%)
  starting transfers between devices  6.66 us (10%)
  between operations  1.39 us (2%)
    pallas_call x1, Pallas kernels, per_device(): pl.pallas_call(functools.partial(filter_kernel, tiles), out_shape=(jax.Sh...  20.7 us
    pallas_call x1, Pallas kernels, per_device(): pl.pallas_call(functools.partial(route_kernel, tiles, cap), out_shape=(ja...  11.9 us
    pallas_call x1, Pallas kernels, per_device(): pl.pallas_call(inner_kernel, out_shape=(middle, middle, jax.ShapeDtypeStr...  11.6 us
    pallas_call x1, Pallas kernels, per_device(): pl.pallas_call(scatter_kernel, out_shape=(edge, edge, jax.ShapeDtypeStruc...  8.8 us
    unnamed x20, local copies, waits for them, and re-layouts  8.34 us
    ppermute x1, starting transfers between devices, per_device(): below = lax.ppermute(high, 'tile', up)  4.59 us
    ppermute x1, starting transfers between devices, per_device(): above = lax.ppermute(low, 'tile', [(j, i) for i, j in up])  2.07 us
  transfers between devices with their start and end apart: 2, of which 0 were waited for; matrix products, arithmetic and copies ran while one was open for 0% of the time, Pallas kernels for 17%

profile of v3, /device:TPU:3, one launch (start us, length us, event | category | flops | bytes accessed | tf_op | source)
XLA Modules:
  0.0 69.4 jit_solution(6406570184346267357)
XLA Ops:
  0.6 11.9 %route.1 = (f32[16,8,512]{2,1,0:T(8,128)}, f32[2,16,256]{2,1,0:T(8,128)}) custom-call(f32[1,4096]{1,0:T(1,128)} %bitcast.12, f32[1,4096]{1,0:T(1,128)} %bitcast.13, s32[1,4096]{1,0:T(1,128)} %bitcast.14, s32[1,4096]{1,0:T(1,128)} %bitcast.15, s32[4,4096]{1,0:T(4,128)} %col_ref.1, f32[4,4096]{1,0:T(4,128)} %itp_ref.1, f32[16,256]{1,0:T(8,128)} %spread_ref.5), custom_call_target="tpu_custom_call" | custom-call | tf_op jit(solution)/shard_map/route/pallas_call | solution.py:463
  12.5 0.0 copy-start.4
  12.5 0.9 %copy-done.4 = f32[16,8,512]{2,1,0:T(8,128)S(1)} copy-done((f32[16,8,512]{2,1,0:T(8,128)S(1)}, f32[16,8,512]{2,1,0:T(8,128)}, u32[]{:S(2)}) %copy-start.4) | copy-done | bytes 262168
  13.5 0.0 copy-start.6
  13.5 0.8 %copy-done.6 = f32[127,127]{1,0:T(8,128)S(1)} copy-done((f32[127,127]{1,0:T(8,128)S(1)}, f32[127,127]{1,0:T(8,128)}, u32[]{:S(2)}) %copy-start.6) | copy-done | bytes 64540
  14.3 8.8 %scatter.1 = (f32[4,128,256]{2,1,0:T(8,128)S(1)}, f32[4,128,256]{2,1,0:T(8,128)S(1)}, f32[33,16,256]{2,1,0:T(8,128)S(1)}, s32[8,128]{1,0:T(8,128)S(1)}, f32[2,2,128,256]{3,2,1,0:T(8,128)S(1)}) custom-call(f32[16,8,512]{2,1,0:T(8,128)S(1)} %copy-done.4, f32[127,127]{1,0:T(8,128)S(1)} %copy-done.6), custom_call_target="tpu_custom_call" | custom-call | tf_op jit(solution)/shard_map/scatter/pallas_call | solution.py:489
  23.1 2.1 %collective-permute-start.1 = (f32[4,128,256]{2,1,0:T(8,128)S(1)}, f32[4,128,256]{2,1,0:T(8,128)S(1)}, u32[]{:S(2)}, u32[]{:S(2)}) collective-permute-start(f32[4,128,256]{2,1,0:T(8,128)S(1)} %get-tuple-element.15.low_ref), channel_id=1, source_target_pairs={{1,0},{2,1},{3,2},{4,3},{5,4},{6,5},{7,6},{8,7},{9,8},{10,9},{11,1... | collective-permute-start | bytes 1572872 | tf_op jit(solution)/shard_map/ppermute | solution.py:513
  25.2 4.6 %collective-permute-start = (f32[4,128,256]{2,1,0:T(8,128)S(1)}, f32[4,128,256]{2,1,0:T(8,128)S(1)}, u32[]{:S(2)}, u32[]{:S(2)}) collective-permute-start(f32[4,128,256]{2,1,0:T(8,128)S(1)} %get-tuple-element.16.high_ref), channel_id=1, source_target_pairs={{0,1},{1,2},{2,3},{3,4},{4,5},{5,6},{6,7},{7,8},{8,9},{9,10},{10,1... | collective-permute-start | bytes 1572872 | tf_op jit(solution)/shard_map/ppermute | solution.py:512
  30.5 0.0 copy-start
  30.5 1.6 %copy-done = f32[127,16,256]{2,1,0:T(8,128)S(1)} copy-done((f32[127,16,256]{2,1,0:T(8,128)S(1)}, f32[127,16,256]{2,1,0:T(8,128)}, u32[]{:S(2)}) %copy-start) | copy-done | bytes 2080792
  32.0 0.0 copy-start.2
  32.0 1.6 %copy-done.2 = f32[127,16,256]{2,1,0:T(8,128)S(1)} copy-done((f32[127,16,256]{2,1,0:T(8,128)S(1)}, f32[127,16,256]{2,1,0:T(8,128)}, u32[]{:S(2)}) %copy-start.2) | copy-done | bytes 2080792
  33.6 0.0 copy-start.5
  33.6 0.7 %copy-done.5 = f32[16,256]{1,0:T(8,128)S(1)} copy-done((f32[16,256]{1,0:T(8,128)S(1)}, f32[16,256]{1,0:T(8,128)}, u32[]{:S(2)}) %copy-start.5) | copy-done | bytes 16408
  34.3 0.8 %copy-done.7 = f32[127,127]{1,0:T(8,128)S(1)} copy-done((f32[127,127]{1,0:T(8,128)S(1)}, f32[127,127]{1,0:T(8,128)}, u32[]{:S(2)}) %copy-start.7) | copy-done | bytes 64540
  35.2 11.6 %inner.1 = (f32[8,128,256]{2,1,0:T(8,128)S(1)}, f32[8,128,256]{2,1,0:T(8,128)S(1)}, f32[8,128]{1,0:T(8,128)S(1)}) custom-call(f32[1]{0:T(128)S(6)} %copy.15.beta_ref, f32[4,128,256]{2,1,0:T(8,128)S(1)} %get-tuple-element.15.low_ref, f32[4,128,256]{2,1,0:T(8,128)S(1)} %get-tuple-element.16.high_ref, f32[33,16,256]{2,1,0:T(8,128)S(1)} %get-tuple-element.17.sort_ref, ...), custom_call_target="tpu_custom_call" | custom-call | flops 10000000000 | bytes 10000000 | tf_op jit(solution)/shard_map/inner/pallas_call | solution.py:514
  46.8 0.0 collective-permute-done.1.above_ref
  46.9 0.0 collective-permute-done.below_ref
  46.9 0.0 copy-done.1
  46.9 0.0 copy-done.3
  46.9 0.0 copy-done.8
  46.9 20.7 %filter.1 = (f32[2032,256]{1,0:T(8,128)S(1)}, f32[2]{0:T(128)S(1)}) custom-call(f32[1]{0:T(128)S(6)} %copy.15.beta_ref, f32[4,128,256]{2,1,0:T(8,128)S(1)} %get-tuple-element.15.low_ref, f32[8,128,256]{2,1,0:T(8,128)S(1)} %get-tuple-element.20.mid_ref, f32[4,128,256]{2,1,0:T(8,128)S(1)} %get-tuple-element.16.high_ref, ...), custom_call_target="tpu_custom_call" | custom-call | tf_op jit(solution)/shard_map/filter/pallas_call | solution.py:532
  67.6 1.3 %copy.16 = f32[127,16,256]{2,1,0:T(8,128)} copy(f32[127,16,256]{2,1,0:T(8,128)S(1)} %bitcast.11) | data formatting | bytes 4161536
  68.9 0.5 copy.17
  (4 shorter events, 0.0 us)
Async XLA Ops:
  12.5 1.0 %copy-start.4 = (f32[16,8,512]{2,1,0:T(8,128)S(1)}, f32[16,8,512]{2,1,0:T(8,128)}, u32[]{:S(2)}) copy-start(f32[16,8,512]{2,1,0:T(8,128)} %get-tuple-element.14.recv_ref) | copy-start | bytes 786436
  13.5 0.8 %copy-start.6 = (f32[127,127]{1,0:T(8,128)S(1)}, f32[127,127]{1,0:T(8,128)}, u32[]{:S(2)}) copy-start(f32[127,127]{1,0:T(8,128)} %root_ref.3) | copy-start | bytes 193552
  23.1 23.7 %collective-permute-start.1 = (f32[4,128,256]{2,1,0:T(8,128)S(1)}, f32[4,128,256]{2,1,0:T(8,128)S(1)}, u32[]{:S(2)}, u32[]{:S(2)}) collective-permute-start(f32[4,128,256]{2,1,0:T(8,128)S(1)} %get-tuple-element.15.low_ref), channel_id=1, source_target_pairs={{1,0},{2,1},{3,2},{4,3},{5,4},{6,5},{7,6},{8,7},{9,8},{10,9},{11,1... | collective-permute-start | bytes 1572872 | tf_op jit(solution)/shard_map/ppermute | solution.py:513
  25.2 21.6 %collective-permute-start = (f32[4,128,256]{2,1,0:T(8,128)S(1)}, f32[4,128,256]{2,1,0:T(8,128)S(1)}, u32[]{:S(2)}, u32[]{:S(2)}) collective-permute-start(f32[4,128,256]{2,1,0:T(8,128)S(1)} %get-tuple-element.16.high_ref), channel_id=1, source_target_pairs={{0,1},{1,2},{2,3},{3,4},{4,5},{5,6},{6,7},{7,8},{8,9},{9,10},{10,1... | collective-permute-start | bytes 1572872 | tf_op jit(solution)/shard_map/ppermute | solution.py:512
  30.5 1.6 %copy-start = (f32[127,16,256]{2,1,0:T(8,128)S(1)}, f32[127,16,256]{2,1,0:T(8,128)}, u32[]{:S(2)}) copy-start(f32[127,16,256]{2,1,0:T(8,128)} %param.19) | copy-start | bytes 6242308
  32.0 1.6 %copy-start.2 = (f32[127,16,256]{2,1,0:T(8,128)S(1)}, f32[127,16,256]{2,1,0:T(8,128)}, u32[]{:S(2)}) copy-start(f32[127,16,256]{2,1,0:T(8,128)} %param.20) | copy-start | bytes 6242308
  33.6 0.7 %copy-start.5 = (f32[16,256]{1,0:T(8,128)S(1)}, f32[16,256]{1,0:T(8,128)}, u32[]{:S(2)}) copy-start(f32[16,256]{1,0:T(8,128)} %spread_ref.5) | copy-start | bytes 49156
  34.3 0.8 %copy-start.7 = (f32[127,127]{1,0:T(8,128)S(1)}, f32[127,127]{1,0:T(8,128)}, u32[]{:S(2)}) copy-start(f32[127,127]{1,0:T(8,128)} %root_ref.3) | copy-start | bytes 193552
  35.2 11.7 %copy-start.1 = (f32[127,16,256]{2,1,0:T(8,128)S(1)}, f32[127,16,256]{2,1,0:T(8,128)}, u32[]{:S(2)}) copy-start(f32[127,16,256]{2,1,0:T(8,128)} %param.19) | copy-start | bytes 6242308
  35.2 11.7 %copy-start.3 = (f32[127,16,256]{2,1,0:T(8,128)S(1)}, f32[127,16,256]{2,1,0:T(8,128)}, u32[]{:S(2)}) copy-start(f32[127,16,256]{2,1,0:T(8,128)} %param.20) | copy-start | bytes 6242308
  35.2 11.7 %copy-start.8 = (f32[2,16,256]{2,1,0:T(8,128)S(1)}, f32[2,16,256]{2,1,0:T(8,128)}, u32[]{:S(2)}) copy-start(f32[2,16,256]{2,1,0:T(8,128)} %get-tuple-element.23.spr_ref) | copy-start | bytes 98308

commit v4 on v3

--- a/solution.py
+++ b/solution.py
@@ -9,13 +9,15 @@
 
 SWEEPS = 4
 GROUP = 256
-WINDOW = 2
+WINDOW = 3
 F32 = jnp.float32
 BF16 = jnp.bfloat16
 HIGH = lax.Precision.HIGHEST
 MESH = pl.DeviceIdType.MESH
-VMEM_LIMIT = 32 * 1024 * 1024
+VMEM_LIMIT = 56 * 1024 * 1024
 ROUTE_LIMIT = 60 * 1024 * 1024
+INNER_LIMIT = 56 * 1024 * 1024
+FILTER_LIMIT = 32 * 1024 * 1024
 
 
 def iota(shape, axis):
@@ -68,10 +70,25 @@
 
 
 def route_kernel(
-    tiles, cap, dep_ref, wgt_ref, own_ref, lev_ref, col_ref, itp_ref, spread_ref, out_ref, spr_ref,
-    left_ref, right_ref, send_ref, send_sem, recv_sem, spr_send, spr_recv,
+    tiles, cap, dep_hbm, wgt_hbm, own_hbm, lev_hbm, col_hbm, itp_hbm, spread_hbm, out_ref, spr_ref,
+    dep_ref, wgt_ref, own_ref, lev_ref, col_ref, itp_ref, spread_ref, load_sem, left_ref, right_ref, send_ref, send_sem, recv_sem, spr_send, spr_recv,
 ):
     me, ens = lax.axis_index("tile"), lax.axis_index("ens")
+    for side, edge in enumerate((0, tiles - 1)):
+
+        @pl.when(me == edge)
+        def _():
+            spr_ref[side] = jnp.zeros(spr_ref.shape[1:], F32)
+
+    loads = [
+        pltpu.make_async_copy(src, dst, load_sem.at[i])
+        for i, (src, dst) in enumerate((
+            (own_hbm, own_ref), (dep_hbm, dep_ref), (wgt_hbm, wgt_ref), (lev_hbm, lev_ref),
+            (col_hbm, col_ref), (itp_hbm, itp_ref), (spread_hbm, spread_ref),
+        ))
+    ]
+    for load in loads:
+        load.start()
     barrier = greet(tiles, me, ens)
     obs = dep_ref.shape[1]
     size = min(256, cap)
@@ -79,6 +96,8 @@
     upper = earlier(size)
     base = jnp.zeros((tiles, 1), F32)
     ones = jnp.ones((16, size), BF16)
+    for load in loads:
+        load.wait()
     for c in range(obs // size):
         at = pl.ds(c * size, size)
         own = own_ref[:, at]
@@ -106,12 +125,6 @@
         for h in range(per):
             k = (t * per + h) * 16
             send_ref[t, :, h * size : (h + 1) * size] = total[k : k + 8] + total[k + 8 : k + 16]
-    for side, edge in enumerate((0, tiles - 1)):
-
-        @pl.when(me == edge)
-        def _():
-            spr_ref[side] = jnp.zeros(spr_ref.shape[1:], F32)
-
     pl.semaphore_wait(barrier, tiles - 1)
 
     def spr_copy(side):
@@ -200,9 +213,11 @@
 
 
 def scatter_kernel(
-    recv_ref, root_ref, low_ref, high_ref, sort_ref, bound_ref, part_ref,
-    left_ref, right_ref, grad_ref, vert_ref, edge_ref, sem,
+    recv_ref, root_hbm, low_ref, high_ref, sort_ref, bound_ref, part_ref,
+    root_ref, root_sem, left_ref, right_ref, grad_ref, vert_ref, edge_ref, sem,
 ):
+    load = pltpu.make_async_copy(root_hbm, root_ref, root_sem)
+    load.start()
     tiles, _, cap = recv_ref.shape
     rows = grad_ref.shape[1]
     wide = SWEEPS
@@ -212,7 +227,6 @@
     per = cap // size
     upper = earlier(size)
     grad_ref[...] = jnp.zeros_like(grad_ref)
-    root = load_root(root_ref, vert_ref)
     ones = jnp.ones((16, GROUP), BF16)
 
     def hot_of(s, c):
@@ -256,6 +270,8 @@
 
     add_rows(0, wide, edge_ref, sort_ref, grad_ref)
     add_rows(rows - wide - 1, rows - 1, edge_ref, sort_ref, grad_ref)
+    load.wait()
+    root = load_root(root_ref, vert_ref)
     for x in range(wide):
         low_ref[x] = levels_of(root, grad_ref, x)
         high_ref[x] = levels_of(root, grad_ref, rows - wide + x)
@@ -306,14 +322,20 @@
 
 
 def inner_kernel(
-    beta_ref, low_ref, high_ref, sort_ref, bound_ref, part_ref, root_ref, spread_ref, lan_hbm, prev_hbm,
-    mid_ref, diff_ref, sum_ref, grad_ref, vert_ref, edge_ref, lan_ref, prev_ref, sem, local_sem,
+    beta_ref, low_ref, high_ref, sort_ref, bound_ref, part_ref, root_hbm, spread_hbm, lan_hbm, prev_hbm,
+    mid_ref, diff_ref, sum_ref, root_ref, spread_ref, small_sem, grad_ref, vert_ref, edge_ref, lan_ref, prev_ref, sem, local_sem,
 ):
     rows = spread_ref.shape[0]
     levels = root_ref.shape[0]
     wide = SWEEPS
     bounds = pltpu.make_async_copy(bound_ref, edge_ref, sem)
     bounds.start()
+    small = [
+        pltpu.make_async_copy(root_hbm, root_ref, small_sem.at[0]),
+        pltpu.make_async_copy(spread_hbm, spread_ref, small_sem.at[1]),
+    ]
+    for load in small:
+        load.start()
     loads = loads_of(((lan_hbm, lan_ref), (prev_hbm, prev_ref)), local_sem)
     for load in loads:
         load.start()
@@ -322,9 +344,11 @@
         grad_ref[dj, rows - wide - 1] = part_ref[1, dj]
         for x in range(wide + 1, rows - wide - 1):
             grad_ref[dj, x] = jnp.zeros(grad_ref.shape[2:], F32)
-    root = load_root(root_ref, vert_ref)
     bounds.wait()
     add_rows(wide, rows - wide - 1, edge_ref, sort_ref, grad_ref)
+    for load in small:
+        load.wait()
+    root = load_root(root_ref, vert_ref)
     for x in range(wide, rows - wide):
         mid_ref[x - wide] = levels_of(root, grad_ref, x)
     for load in loads:
@@ -349,18 +373,19 @@
 
 
 def filter_kernel(
-    tiles, beta_ref, low_ref, mid_ref, high_ref, below_ref, above_ref, inner_ref, part_ref, spread_ref, spr_ref,
-    lan_hbm, prev_hbm, out_hbm, coef_ref,
+    tiles, beta_ref, low_ref, mid_ref, high_ref, below_ref, above_ref, inner_ref, part_ref, spread_hbm, spr_ref,
+    lan_hbm, prev_hbm, out_hbm, coef_ref, spread_ref, spread_sem,
     lan_ref, prev_ref, diff_ref, sum_ref, all_ref, local_sem, sum_send, sum_recv,
 ):
     me, ens = lax.axis_index("tile"), lax.axis_index("ens")
     rows, width = spread_ref.shape
     levels = lan_hbm.shape[0] // rows
     wide = SWEEPS
-    barrier = greet(tiles, me, ens)
-    loads = loads_of(((lan_hbm, lan_ref), (prev_hbm, prev_ref)), local_sem)
+    loads = [pltpu.make_async_copy(spread_hbm, spread_ref, spread_sem)]
+    loads += loads_of(((lan_hbm, lan_ref), (prev_hbm, prev_ref)), local_sem)
     for load in loads:
         load.start()
+    barrier = greet(tiles, me, ens)
     for load in loads:
         load.wait()
     beta_prev = beta_ref[0]
@@ -459,6 +484,7 @@
     vmem = pl.BlockSpec(memory_space=pltpu.VMEM)
     smem = pl.BlockSpec(memory_space=pltpu.SMEM)
     hbm = pl.BlockSpec(memory_space=pl.ANY)
+    far = pl.BlockSpec(memory_space=pltpu.HBM)
     dma = pltpu.SemaphoreType.DMA
     received, spread_halo = pl.pallas_call(
         functools.partial(route_kernel, tiles, cap),
@@ -466,9 +492,17 @@
             jax.ShapeDtypeStruct((tiles, 8, cap), F32),
             jax.ShapeDtypeStruct((2, rows, width), F32),
         ),
-        in_specs=[vmem] * 7,
+        in_specs=[far] * 7,
         out_specs=(vmem, vmem),
         scratch_shapes=[
+            pltpu.VMEM((1, obs), F32),
+            pltpu.VMEM((1, obs), F32),
+            pltpu.VMEM((1, obs), jnp.int32),
+            pltpu.VMEM((1, obs), jnp.int32),
+            pltpu.VMEM(columns.shape, jnp.int32),
+            pltpu.VMEM(interp_weight.shape, F32),
+            pltpu.VMEM(spread.shape, F32),
+            dma((7,)),
             pltpu.VMEM((tiles * cap // size * 16, obs), BF16),
             pltpu.VMEM((size, obs), BF16),
             pltpu.VMEM((tiles, 8, cap), F32),
@@ -495,9 +529,11 @@
             jax.ShapeDtypeStruct((8, 128), jnp.int32),
             jax.ShapeDtypeStruct((2, 2, 128, width), F32),
         ),
-        in_specs=[vmem] * 2,
+        in_specs=[vmem, far],
         out_specs=[vmem] * 5,
         scratch_shapes=[
+            pltpu.VMEM(vert_root.shape, F32),
+            dma,
             pltpu.VMEM((slots // GROUP * 16, slots), BF16),
             pltpu.VMEM((GROUP, slots), BF16),
             pltpu.VMEM((2, rows, 128, width), F32),
@@ -514,9 +550,12 @@
     mid, inner, sums = pl.pallas_call(
         inner_kernel,
         out_shape=(middle, middle, jax.ShapeDtypeStruct((8, 128), F32)),
-        in_specs=[smem] + [vmem] * 7 + [hbm] * 2,
+        in_specs=[smem] + [vmem] * 5 + [far] * 4,
         out_specs=[vmem] * 3,
         scratch_shapes=[
+            pltpu.VMEM(vert_root.shape, F32),
+            pltpu.VMEM(spread.shape, F32),
+            dma((2,)),
             pltpu.VMEM((2, rows, 128, width), F32),
             pltpu.VMEM((128, 128), F32),
             pltpu.SMEM((8, 128), jnp.int32),
@@ -525,16 +564,18 @@
             dma,
             dma((2, width // 128)),
         ],
-        compiler_params=pltpu.CompilerParams(vmem_limit_bytes=VMEM_LIMIT),
+        compiler_params=pltpu.CompilerParams(vmem_limit_bytes=INNER_LIMIT),
         cost_estimate=pl.CostEstimate(flops=10**10, bytes_accessed=10**7, transcendentals=0),
         name="inner",
     )(beta_prev, low, high, order, bound, part, vert_root, spread, lan, prev)
     vector, coefficients = pl.pallas_call(
         functools.partial(filter_kernel, tiles),
         out_shape=(jax.ShapeDtypeStruct(flat, F32), jax.ShapeDtypeStruct((2,), F32)),
-        in_specs=[smem] + [vmem] * 9 + [hbm] * 2,
+        in_specs=[smem] + [vmem] * 7 + [far] + [vmem] + [far] * 2,
         out_specs=(hbm, smem),
         scratch_shapes=[
+            pltpu.VMEM(spread.shape, F32),
+            dma,
             pltpu.VMEM((width // 128, levels * rows, 128), F32),
             pltpu.VMEM((width // 128, levels * rows, 128), F32),
             pltpu.VMEM((2 * SWEEPS, 128, width), F32),
@@ -544,7 +585,7 @@
             dma((tiles,)), dma((tiles,)),
         ],
         compiler_params=pltpu.CompilerParams(
-            collective_id=1, has_side_effects=True, vmem_limit_bytes=VMEM_LIMIT
+            collective_id=1, has_side_effects=True, vmem_limit_bytes=FILTER_LIMIT
         ),
         name="filter",
     )(beta_prev, low, mid, high, below, above, inner, sums, spread, spread_halo, lan, prev)

time: 70.1 us -> 67 us (0.956)
  the two profiles are of different devices: /device:TPU:3 before, /device:TPU:0 now
where the time goes in v4:
time: 67 us; the launch traced here: 66.7 us
  Pallas kernels  55.8 us (83%)
  local copies, waits for them, and re-layouts  4.98 us (7%)
  starting transfers between devices  4.37 us (7%)
  between operations  1.45 us (2%)
    pallas_call x1, Pallas kernels, per_device(): pl.pallas_call(functools.partial(filter_kernel, tiles), out_shape=(jax.Sh...  16 us
    pallas_call x1, Pallas kernels, per_device(): pl.pallas_call(inner_kernel, out_shape=(middle, middle, jax.ShapeDtypeStr...  15.3 us
    pallas_call x1, Pallas kernels, per_device(): pl.pallas_call(functools.partial(route_kernel, tiles, cap), out_shape=(ja...  12.8 us
    pallas_call x1, Pallas kernels, per_device(): pl.pallas_call(scatter_kernel, out_shape=(edge, edge, jax.ShapeDtypeStruc...  11.7 us
    unnamed x20, local copies, waits for them, and re-layouts  4.98 us
    ppermute x1, starting transfers between devices, per_device(): below = lax.ppermute(high, 'tile', up)  3.08 us
  transfers between devices with their start and end apart: 2, of which 0 were waited for; matrix products, arithmetic and copies ran while one was open for 0% of the time, Pallas kernels for 23%

profile of v4, /device:TPU:0, one launch (start us, length us, event | category | flops | bytes accessed | tf_op | source)
XLA Modules:
  0.0 66.7 jit_solution(15945352244078047974)
XLA Ops:
  0.6 12.8 %route.1 = (f32[16,8,512]{2,1,0:T(8,128)}, f32[2,16,256]{2,1,0:T(8,128)}) custom-call(f32[1,4096]{1,0:T(1,128)} %bitcast.12, f32[1,4096]{1,0:T(1,128)} %bitcast.13, s32[1,4096]{1,0:T(1,128)} %bitcast.14, s32[1,4096]{1,0:T(1,128)} %bitcast.15, s32[4,4096]{1,0:T(4,128)} %col_hbm.1, f32[4,4096]{1,0:T(4,128)} %itp_hbm.1, f32[16,256]{1,0:T(8,128)} %spread_hbm.5), custom_call_target="tpu_custom_call" | custom-call | tf_op jit(solution)/shard_map/route/pallas_call | solution.py:489
  13.4 11.7 %scatter.1 = (f32[4,128,256]{2,1,0:T(8,128)}, f32[4,128,256]{2,1,0:T(8,128)}, f32[34,16,256]{2,1,0:T(8,128)}, s32[8,128]{1,0:T(8,128)}, f32[2,2,128,256]{3,2,1,0:T(8,128)}) custom-call(f32[16,8,512]{2,1,0:T(8,128)} %get-tuple-element.14.recv_ref, f32[127,127]{1,0:T(8,128)} %root_hbm.3), custom_call_target="tpu_custom_call" | custom-call | tf_op jit(solution)/shard_map/scatter/pallas_call | solution.py:523
  25.2 1.3 %collective-permute-start.1 = (f32[4,128,256]{2,1,0:T(8,128)}, f32[4,128,256]{2,1,0:T(8,128)S(1)}, u32[]{:S(2)}, u32[]{:S(2)}) collective-permute-start(f32[4,128,256]{2,1,0:T(8,128)} %get-tuple-element.15.low_ref), channel_id=1, source_target_pairs={{1,0},{2,1},{3,2},{4,3},{5,4},{6,5},{7,6},{8,7},{9,8},{10,9},{11,1... | collective-permute-start | bytes 1572872 | tf_op jit(solution)/shard_map/ppermute | solution.py:549
  26.5 3.1 %collective-permute-start = (f32[4,128,256]{2,1,0:T(8,128)}, f32[4,128,256]{2,1,0:T(8,128)S(1)}, u32[]{:S(2)}, u32[]{:S(2)}) collective-permute-start(f32[4,128,256]{2,1,0:T(8,128)} %get-tuple-element.16.high_ref), channel_id=1, source_target_pairs={{0,1},{1,2},{2,3},{3,4},{4,5},{5,6},{6,7},{7,8},{8,9},{9,10},{10,1... | collective-permute-start | bytes 1572872 | tf_op jit(solution)/shard_map/ppermute | solution.py:548
  30.2 0.0 copy-start
  30.2 0.0 copy-start.1
  30.3 0.0 copy-start.6
  30.3 0.0 copy-start.7
  30.3 15.3 %inner.1 = (f32[8,128,256]{2,1,0:T(8,128)}, f32[8,128,256]{2,1,0:T(8,128)}, f32[8,128]{1,0:T(8,128)}) custom-call(f32[1]{0:T(128)S(6)} %copy.15.beta_ref, f32[4,128,256]{2,1,0:T(8,128)} %get-tuple-element.15.low_ref, f32[4,128,256]{2,1,0:T(8,128)} %get-tuple-element.16.high_ref, f32[34,16,256]{2,1,0:T(8,128)} %get-tuple-element.17.sort_ref, ...), custom_call_target="tpu_custom_call" | custom-call | flops 10000000000 | bytes 10000000 | tf_op jit(solution)/shard_map/inner/pallas_call | solution.py:550
  45.6 0.0 collective-permute-done.1.above_ref
  45.6 0.0 collective-permute-done.below_ref
  45.6 0.0 copy-done
  45.6 0.0 copy-done.1
  45.6 0.0 copy-done.4
  45.6 0.0 copy-done.5
  45.6 0.0 copy-done.6
  45.6 0.0 copy-done.7
  45.7 0.0 copy-start.2
  45.7 1.2 %copy-done.2 = f32[8,128,256]{2,1,0:T(8,128)S(1)} copy-done((f32[8,128,256]{2,1,0:T(8,128)S(1)}, f32[8,128,256]{2,1,0:T(8,128)}, u32[]{:S(2)}) %copy-start.2) | copy-done | bytes 1048600
  46.9 1.2 %copy-done.3 = f32[8,128,256]{2,1,0:T(8,128)S(1)} copy-done((f32[8,128,256]{2,1,0:T(8,128)S(1)}, f32[8,128,256]{2,1,0:T(8,128)}, u32[]{:S(2)}) %copy-start.3) | copy-done | bytes 1048600
  48.1 0.7 %copy-done.8 = f32[8,128]{1,0:T(8,128)S(1)} copy-done((f32[8,128]{1,0:T(8,128)S(1)}, f32[8,128]{1,0:T(8,128)}, u32[]{:S(2)}) %copy-start.8) | copy-done | bytes 4120
  48.8 16.0 %filter.1 = (f32[2032,256]{1,0:T(8,128)S(1)}, f32[2]{0:T(128)S(1)}) custom-call(f32[1]{0:T(128)S(6)} %copy.15.beta_ref, f32[4,128,256]{2,1,0:T(8,128)S(1)} %copy-done.4, f32[8,128,256]{2,1,0:T(8,128)S(1)} %copy-done.2, f32[4,128,256]{2,1,0:T(8,128)S(1)} %copy-done.5, f32[4,128,256]{2,1,0:T(8,128)S(1)} %collective-permute-done.below_ref, ...), custom_call_target="tpu_custom_call" | custom-call | tf_op jit(solution)/shard_map/filter/pallas_call | solution.py:571
  64.8 1.3 %copy.16 = f32[127,16,256]{2,1,0:T(8,128)} copy(f32[127,16,256]{2,1,0:T(8,128)S(1)} %bitcast.11) | data formatting | bytes 4161536
  66.1 0.5 copy.17
  (4 shorter events, 0.0 us)
Async XLA Ops:
  25.2 20.4 %collective-permute-start.1 = (f32[4,128,256]{2,1,0:T(8,128)}, f32[4,128,256]{2,1,0:T(8,128)S(1)}, u32[]{:S(2)}, u32[]{:S(2)}) collective-permute-start(f32[4,128,256]{2,1,0:T(8,128)} %get-tuple-element.15.low_ref), channel_id=1, source_target_pairs={{1,0},{2,1},{3,2},{4,3},{5,4},{6,5},{7,6},{8,7},{9,8},{10,9},{11,1... | collective-permute-start | bytes 1572872 | tf_op jit(solution)/shard_map/ppermute | solution.py:549
  26.5 19.1 %collective-permute-start = (f32[4,128,256]{2,1,0:T(8,128)}, f32[4,128,256]{2,1,0:T(8,128)S(1)}, u32[]{:S(2)}, u32[]{:S(2)}) collective-permute-start(f32[4,128,256]{2,1,0:T(8,128)} %get-tuple-element.16.high_ref), channel_id=1, source_target_pairs={{0,1},{1,2},{2,3},{3,4},{4,5},{5,6},{6,7},{7,8},{8,9},{9,10},{10,1... | collective-permute-start | bytes 1572872 | tf_op jit(solution)/shard_map/ppermute | solution.py:548
  30.2 15.4 %copy-start = (f32[127,16,256]{2,1,0:T(8,128)S(1)}, f32[127,16,256]{2,1,0:T(8,128)}, u32[]{:S(2)}) copy-start(f32[127,16,256]{2,1,0:T(8,128)} %param.19) | copy-start | bytes 6242308
  30.2 15.4 %copy-start.1 = (f32[127,16,256]{2,1,0:T(8,128)S(1)}, f32[127,16,256]{2,1,0:T(8,128)}, u32[]{:S(2)}) copy-start(f32[127,16,256]{2,1,0:T(8,128)} %param.20) | copy-start | bytes 6242308
  30.2 15.4 %copy-start.4 = (f32[4,128,256]{2,1,0:T(8,128)S(1)}, f32[4,128,256]{2,1,0:T(8,128)}, u32[]{:S(2)}) copy-start(f32[4,128,256]{2,1,0:T(8,128)} %get-tuple-element.15.low_ref) | copy-start | bytes 1572868
  30.2 15.4 %copy-start.5 = (f32[4,128,256]{2,1,0:T(8,128)S(1)}, f32[4,128,256]{2,1,0:T(8,128)}, u32[]{:S(2)}) copy-start(f32[4,128,256]{2,1,0:T(8,128)} %get-tuple-element.16.high_ref) | copy-start | bytes 1572868
  30.3 15.4 %copy-start.6 = (f32[16,256]{1,0:T(8,128)S(1)}, f32[16,256]{1,0:T(8,128)}, u32[]{:S(2)}) copy-start(f32[16,256]{1,0:T(8,128)} %spread_hbm.5) | copy-start | bytes 49156
  30.3 15.4 %copy-start.7 = (f32[2,16,256]{2,1,0:T(8,128)S(1)}, f32[2,16,256]{2,1,0:T(8,128)}, u32[]{:S(2)}) copy-start(f32[2,16,256]{2,1,0:T(8,128)} %get-tuple-element.23.spr_ref) | copy-start | bytes 98308
  45.7 1.2 %copy-start.2 = (f32[8,128,256]{2,1,0:T(8,128)S(1)}, f32[8,128,256]{2,1,0:T(8,128)}, u32[]{:S(2)}) copy-start(f32[8,128,256]{2,1,0:T(8,128)} %get-tuple-element.20.mid_ref) | copy-start | bytes 3145732
  46.9 1.2 %copy-start.3 = (f32[8,128,256]{2,1,0:T(8,128)S(1)}, f32[8,128,256]{2,1,0:T(8,128)}, u32[]{:S(2)}) copy-start(f32[8,128,256]{2,1,0:T(8,128)} %get-tuple-element.21.inner_ref) | copy-start | bytes 3145732
  48.1 0.7 %copy-start.8 = (f32[8,128]{1,0:T(8,128)S(1)}, f32[8,128]{1,0:T(8,128)}, u32[]{:S(2)}) copy-start(f32[8,128]{1,0:T(8,128)} %get-tuple-element.22.part_ref) | copy-start | bytes 12292
